TPU v7x, 256 devices: a whole 4x4x8 slice. The times are simulated.
256 devices in a mesh: band: 4 (over x_lo, core), space: 64 (over x_hi, y, z).
Axes of the slice: x: 4 (x_hi: 2, x_lo: 2; x = x_hi * 2 + x_lo), y: 4, z: 8, core: 2. Of those that a mesh axis runs over, the one named last changes fastest.
Arguments:
- orbitals: bfloat16 [96, 1024, 16, 128], P('band', 'space'), may hold values from -0.796875 to 0.796875
- occupations: float32 [96], P('band'), may hold values from 0.5 to 2
- potential_in: float32 [1024, 16, 128], P('space'), may hold values from -6 to 6
- ionic_potential: float32 [1024, 16, 128], P('space'), may hold values from -6 to 6
- hartree_prev: float32 [1024, 16, 128], P('space'), may hold values from -6 to 6
- projectors: bfloat16 [512, 13, 16, 256], P('space'), may hold values from -0.375 to 0.375
- box_start: int32 [3, 512], replicated, may hold values from 0 to 1023, as said below
- coupling: float32 [13, 13], replicated, may hold values from -6 to 6
Outputs:
- applied: bfloat16 [96, 1024, 16, 128], P('band', 'space')
- potential: float32 [1024, 16, 128], P('space')
Inputs may be any that keep to these rules, and one draw needn't show every extreme that they name: `box_start`: column a holds the first plane, row and column of atom a's box. The plane lies among the 16 planes that begin at (a // 8) * 16; the row is at most 0 and the column at most 112. Atom 0's box begins at plane, row and column 0, and the last atom's box begins on plane 1024 - 1.
All inputs are finite; a program needn't handle non-finite values.
Results may differ from a plain program's by a relative error of at most 0.013.
Values may be sent and summed in bfloat16 or wider, within the bound.
A program may use at most 128 MiB of HBM per device.

v0:
```python
import math

import jax
import jax.numpy as jnp
from jax import lax
from jax.sharding import Mesh
from jax.sharding import PartitionSpec as P

SWEEPS = 2
SPACE = ("space_0", "space_1", "space_2")
BAND = ("band_0", "band_1")
BAND_SPACE = ("band_0", "band_1", "space_0", "space_1", "space_2")


screening = 0.25
four_pi = 4.0 * math.pi
stencil_far = ((1, 4.0 / 3.0), (2, -1.0 / 12.0))


def padded(cells, sides, width):
    for axis, dim in sides:
        count = lax.axis_size(axis)
        head = lax.slice_in_dim(cells, 0, width, axis=dim)
        tail = lax.slice_in_dim(cells, cells.shape[dim] - width, cells.shape[dim], axis=dim)
        cells = jnp.concatenate(
            [
                lax.ppermute(tail, axis, [(i, (i + 1) % count) for i in range(count)]),
                cells,
                lax.ppermute(head, axis, [((i + 1) % count, i) for i in range(count)]),
            ],
            axis=dim,
        )
    return cells


def from_behind(block, axis, distance):
    devices = range(lax.axis_size(axis))
    route = [((i - distance) % len(devices), i) for i in devices]
    return lax.ppermute(block, axis, route)


def copy_for_each(array, axis):
    count = lax.axis_size(axis)
    return lax.all_to_all(
        jnp.broadcast_to(array[None], (count, *array.shape)), axis, 0, 0, tiled=True
    )


def of_everyone(array, axis):
    return copy_for_each(array, axis).astype(jnp.float32).sum(axis=0)


def by_axis(array, axes):
    for axis in axes:
        array = lax.psum(array, axis)
    return array


def embed_atom(beta_atom, row, column, rows_y, cols_z):
    nproj_here, width, square = beta_atom.shape
    steps_box = jnp.arange(width, dtype=jnp.int32)
    row_hot = (jnp.arange(rows_y, dtype=jnp.int32)[None, :] == (row + steps_box)[:, None]).astype(
        jnp.float32
    )
    col_hot = (
        jnp.arange(cols_z, dtype=jnp.int32)[None, :] == (column + steps_box)[:, None]
    ).astype(jnp.float32)
    cube = beta_atom.astype(jnp.float32).reshape(nproj_here, width, width, width)
    placed = jnp.einsum("pijk,kz->pijz", cube, col_hot, precision=lax.Precision.HIGHEST)
    placed = jnp.einsum("pijz,jy->piyz", placed, row_hot, precision=lax.Precision.HIGHEST)
    return placed.astype(jnp.bfloat16)


def gather_coefficients(field, beta_block, starts, row_start, col_start):
    rows_y = field.shape[2]
    cols_z = field.shape[3]
    width = beta_block.shape[2]

    def per_atom(inputs):
        beta_atom, plane, row, column = inputs
        placed = embed_atom(beta_atom, row, column, rows_y, cols_z)
        slab = lax.dynamic_slice_in_dim(field, plane, width, 1)
        return jnp.einsum("piyz,oiyz->po", placed, slab, preferred_element_type=jnp.float32)

    return lax.map(per_atom, (beta_block, starts, row_start, col_start))


def weigh(coupling, coefficients):
    return jnp.einsum(
        "pq,aqo->apo", coupling, coefficients, precision=lax.Precision.HIGHEST
    ).astype(jnp.bfloat16)


def deposit(buffer, beta_block, weighted, starts, row_start, col_start):
    rows_y = buffer.shape[2]
    cols_z = buffer.shape[3]
    width = beta_block.shape[2]

    def add_atom(atom_index, summed):
        placed = embed_atom(
            beta_block[atom_index], row_start[atom_index], col_start[atom_index], rows_y, cols_z
        )
        update = jnp.einsum(
            "piyz,po->oiyz", placed, weighted[atom_index], preferred_element_type=jnp.float32
        )
        plane = starts[atom_index]
        current = lax.dynamic_slice_in_dim(summed, plane, width, 1)
        return lax.dynamic_update_slice_in_dim(summed, current + update, plane, 1)

    return lax.fori_loop(0, beta_block.shape[0], add_atom, buffer)


def relax_slab(field, source_ext, margin):
    inner = field[1:-1]
    neighbours = field[2:] + field[:-2]
    neighbours = neighbours + jnp.roll(inner, 1, 1) + jnp.roll(inner, -1, 1)
    neighbours = neighbours + jnp.roll(inner, 1, 2) + jnp.roll(inner, -1, 2)
    total = source_ext.shape[0]
    cropped = source_ext[margin : total - margin]
    return (neighbours + cropped) / (6.0 + screening)


def local(
    orbitals,
    occupations,
    potential_in,
    ionic_potential,
    hartree_prev,
    projectors,
    box_start,
    coupling,
):
    orbit_count, planes, rows_y, cols_z = orbitals.shape
    atoms_dev = projectors.shape[0]
    n_space = lax.axis_size(SPACE)
    domain = lax.axis_index(SPACE)
    center = orbitals.astype(jnp.float32)
    extended = padded(orbitals, ((SPACE, 1),), 2)
    laplacian = -7.5 * center
    for distance, weight in stencil_far:
        upper = extended[:, 2 + distance : 2 + distance + planes].astype(jnp.float32)
        lower = extended[:, 2 - distance : 2 - distance + planes].astype(jnp.float32)
        laplacian = laplacian + weight * (upper + lower)
        for dimension in (2, 3):
            laplacian = laplacian + weight * (
                jnp.roll(center, distance, dimension) + jnp.roll(center, -distance, dimension)
            )
    local_cols = lax.dynamic_slice_in_dim(box_start, domain * atoms_dev, atoms_dev, 1)
    local_offset = local_cols[0] % planes
    following = from_behind(orbitals, SPACE, -1)
    joined = jnp.concatenate([orbitals, following], axis=1)
    coefficients = gather_coefficients(
        joined, projectors, local_offset, local_cols[1], local_cols[2]
    )
    weighted = weigh(coupling, coefficients)
    buffer = jnp.zeros((orbit_count, 2 * planes, rows_y, cols_z), jnp.float32)
    buffer = deposit(buffer, projectors, weighted, local_offset, local_cols[1], local_cols[2])
    carried = from_behind(buffer[:, planes:], SPACE, 1)
    nonlocal_part = buffer[:, :planes] + carried
    applied = (-0.5 * laplacian + potential_in[None] * center + nonlocal_part).astype(jnp.bfloat16)
    partial_density = jnp.sum(occupations[:, None, None, None] * center * center, axis=0)
    cell_count = planes * rows_y * cols_z * n_space
    density = of_everyone(partial_density.astype(jnp.bfloat16), BAND).astype(jnp.float32)
    charge_total = by_axis(jnp.sum(partial_density), BAND_SPACE)
    source = four_pi * (density - charge_total / cell_count)
    hartree = hartree_prev
    stacked = jnp.stack([hartree, source])
    wide = padded(stacked.astype(jnp.bfloat16), ((SPACE, 1),), SWEEPS).astype(stacked.dtype)
    field = wide[0]
    source_ext = wide[1]
    for sweep_index in range(SWEEPS):
        field = relax_slab(field, source_ext, sweep_index + 1)
    hartree = field
    potential = ionic_potential + hartree - jnp.cbrt(3.0 * density / math.pi)
    return (applied, potential)


def solution(mesh):
    torus = Mesh(
        mesh.devices.reshape(2, 2, 2, 4, 8), ("band_0", "band_1", "space_0", "space_1", "space_2")
    )
    return jax.shard_map(
        local,
        mesh=torus,
        in_specs=(
            P(BAND, SPACE, None, None),
            P(BAND),
            P(SPACE, None, None),
            P(SPACE, None, None),
            P(SPACE, None, None),
            P(SPACE, None, None, None),
            P(),
            P(),
        ),
        out_specs=(P(BAND, SPACE, None, None), P(SPACE, None, None)),
        check_vma=False,
    )
```

profile of v0, /device:TPU:24, one launch (start us, length us, event | category | flops | bytes accessed | tf_op | source)
XLA Modules:
  0.0 400.7 jit_solution(7138773816324284304)
XLA Ops:
  0.7 3.1 fusion.45
  4.5 4.0 %all-to-all-start = ((bf16[4,16,16,128]{3,2,1,0:T(8,128)(2,1)}), bf16[4,16,16,128]{3,2,1,0:T(8,128)(2,1)}, u32[]{:S(2)}, u32[]{:S(2)}) async-start(bf16[4,16,16,128]{3,2,1,0:T(8,128)(2,1)} %broadcast_in_dim.36), calls=%async_computation | async-start | bytes 524288 | tf_op jit(solution)/shard_map/all_to_all | solution.py:44
  8.5 1.8 fusion.66
  10.4 6.0 %collective-permute-start = (bf16[24,2,16,128]{3,2,1,0:T(8,128)(2,1)}, bf16[24,2,16,128]{3,2,1,0:T(8,128)(2,1)}, u32[]{:S(2)}, u32[]{:S(2)}) collective-permute-start(bf16[24,2,16,128]{3,2,1,0:T(8,128)(2,1)} %get-tuple-element.195), channel_id=1, source_target_pairs={{1,0},{2,1},{3,2},{4,3},{5,4},{6,5},{7,6},{8,7},{9,8},{10,9},{11,1... | collective-permute-start | bytes 589832 | tf_op jit(solution)/shard_map/ppermute | solution.py:29
  16.4 1.0 copy.15
  17.5 4.2 %collective-permute-start.2 = (bf16[24,16,16,128]{3,0,2,1:T(8,128)(2,1)S(1)}, bf16[24,16,16,128]{3,0,2,1:T(8,128)(2,1)}, u32[]{:S(2)}, u32[]{:S(2)}) collective-permute-start(bf16[24,16,16,128]{3,0,2,1:T(8,128)(2,1)S(1)} %copy.15), channel_id=1, source_target_pairs={{1,0},{2,1},{3,2},{4,3},{5,4},{6,5},{7,6},{8,7},{9,8},{10,9},{11,1... | collective-permute-start | bytes 4718600 | tf_op jit(solution)/shard_map/ppermute | solution.py:39
  22.7 1.3 fusion.70
  24.0 3.5 fusion.73
  27.5 3.3 fusion.72
  30.8 3.3 fusion.71
  34.0 3.6 fusion.69
  37.6 5.5 %psum.35 = f32[]{:T(128)} all-reduce(f32[]{:T(128)} %get-tuple-element.165), channel_id=1, replica_groups=mesh['band_0'=2,'band_1'=2,'space_0'=2,'space_1'=4,'space_2'=8] {'band_0'}, use_global_device_ids=true, to_apply=%region_7.8 | all-reduce | flops 1 | bytes 8 | tf_op jit(solution)/shard_map/psum | solution.py:55
  43.1 3.1 psum.36
  46.2 7.1 %psum.37 = f32[]{:T(128)} all-reduce(f32[]{:T(128)} %psum.36), channel_id=1, replica_groups=mesh['band_0'=2,'band_1'=2,'space_0'=2,'space_1'=4,'space_2'=8] {'space_0'}, use_global_device_ids=true, to_apply=%region_9.10 | all-reduce | flops 1 | bytes 8 | tf_op jit(solution)/shard_map/psum | solution.py:55
  53.3 15.7 %psum.38 = f32[]{:T(128)} all-reduce(f32[]{:T(128)} %psum.37), channel_id=1, replica_groups=mesh['band_0'=2,'band_1'=2,'space_0'=2,'space_1'=4,'space_2'=8] {'space_1'}, use_global_device_ids=true, to_apply=%region_10.11 | all-reduce | flops 1 | bytes 8 | tf_op jit(solution)/shard_map/psum | solution.py:55
  69.0 21.4 %psum.39 = f32[]{:T(128)} all-reduce(f32[]{:T(128)} %psum.38), channel_id=1, replica_groups=mesh['band_0'=2,'band_1'=2,'space_0'=2,'space_1'=4,'space_2'=8] {'space_2'}, use_global_device_ids=true, to_apply=%region_11.12 | all-reduce | flops 1 | bytes 8 | tf_op jit(solution)/shard_map/psum | solution.py:55
  91.8 3.4 fusion.67
  95.2 3.3 fusion.68
  99.5 3.3 pad_maximum_fusion
  102.9 72.5 %while.23 = (s32[]{:T(128)}, f32[8,13,24]{2,1,0:T(8,128)S(1)}, s32[8]{0:T(128)S(1)}, bf16[8,13,16,256]{3,2,1,0:T(8,128)(2,1)}, s32[8]{0:T(128)S(1)}, /*index=5*/...) while((s32[]{:T(128)}, f32[8,13,24]{2,1,0:T(8,128)S(1)}, ...), condition=%wide.region_1.2_spmd, body=%wide.region_0.1_spmd.sunk | while | flops 115869984 | bytes 19808740 | solution.py:85
  109.8 1.0 fusion.112
  128.0 1.0 fusion.112
  137.0 1.0 fusion.112
  155.2 1.0 fusion.112
  175.6 3.4 broadcast_in_dim.34.clone
  179.0 132.7 %while.24 = (s32[]{:T(128)}, f32[24,32,16,128]{3,2,1,0:T(8,128)}, s32[8]{0:T(128)S(1)}, bf16[8,13,24]{2,1,0:T(8,128)(2,1)S(1)}, s32[8]{0:T(128)S(1)}, /*index=5*...) while((s32[]{:T(128)}, f32[24,32,16,128]{3,2,1,0:T(8,128)}, ...), condition=%wide.region_3.4_spmd, body=%wide.region_2.3_spmd.sunk | while | flops 116656416 | bytes 68563480 | solution.py:110
  187.0 2.5 constant_dynamic-slice_fusion.8
  189.4 2.3 copy_add_fusion.2
  191.8 1.1 copy_dynamic-update-slice_fusion.2
  192.9 2.6 copy-done.3
  203.5 2.5 constant_dynamic-slice_fusion.8
  206.0 2.3 copy_add_fusion.2
  208.4 1.1 copy_dynamic-update-slice_fusion.2
  209.5 2.6 copy-done.3
  220.1 2.5 constant_dynamic-slice_fusion.8
  222.6 2.3 copy_add_fusion.2
  225.0 1.1 copy_dynamic-update-slice_fusion.2
  226.1 2.6 copy-done.3
  236.7 2.5 constant_dynamic-slice_fusion.8
  239.2 2.3 copy_add_fusion.2
  241.6 1.1 copy_dynamic-update-slice_fusion.2
  242.7 2.6 copy-done.3
  253.3 2.5 constant_dynamic-slice_fusion.8
  255.8 2.3 copy_add_fusion.2
  258.2 1.1 copy_dynamic-update-slice_fusion.2
  259.3 2.6 copy-done.3
  269.9 2.5 constant_dynamic-slice_fusion.8
  272.4 2.3 copy_add_fusion.2
  274.7 1.1 copy_dynamic-update-slice_fusion.2
  275.9 2.6 copy-done.3
  286.5 2.5 constant_dynamic-slice_fusion.8
  289.0 2.3 copy_add_fusion.2
  291.3 1.1 copy_dynamic-update-slice_fusion.2
  292.5 2.6 copy-done.3
  303.1 2.5 constant_dynamic-slice_fusion.8
  305.5 2.3 copy_add_fusion.2
  307.9 1.1 copy_dynamic-update-slice_fusion.2
  309.0 2.6 copy-done.3
  311.7 2.4 slice.247
  314.9 3.6 collective-permute-start.5
  320.3 1.3 constant_dynamic-update-slice_fusion
  321.6 59.4 %collective-permute-done.4 = bf16[2,2,16,128]{3,2,1,0:T(8,128)(2,1)S(1)} collective-permute-done((bf16[2,2,16,128]{3,2,1,0:T(8,128)(2,1)S(1)}, bf16[2,2,16,128]{3,2,1,0:T(8,128)(2,1)S(1)}, u32[]{:S(2)}, u32[]{:S(2)}) %collective-permute-start.4) | collective-permute-done | bytes 16416 | tf_op jit(solution)/shard_map/ppermute | solution.py:27
  382.7 1.8 copy-done.8
  384.7 15.7 %fusion.41 = bf16[24,16,16,128]{3,2,1,0:T(8,128)(2,1)} fusion(f32[24,16,15,128]{3,2,1,0:T(8,128)S(1)} %copy-done.6, f32[24,16,1,128]{3,2,1,0:T(1,128)} %get-tuple-element.214, f32[24,16,1,128]{3,2,1,0:T(1,128)} %get-tuple-element.213, f32[24,16,15,128]{3,2,1,0:T(8,128)S(1)} %copy-done.5, f32[24,16,16,127]{3,2,1,0:T(8,128)} %get-tuple-element.208, ...), kind=kLoop, calls=%fused_computation.48 | loop fusion | flops 29884416 | bytes 41025536 | tf_op jit(solution)/shard_map/convert_element_type | solution.py:160
  (272 shorter events, 108.6 us)
Async XLA Ops:
  0.6 174.8 %copy-start = (f32[13,13]{1,0:T(8,128)S(1)}, f32[13,13]{1,0:T(8,128)}, u32[]{:S(2)}) copy-start(f32[13,13]{1,0:T(8,128)} %param.19) | copy-start | bytes 2032
  0.6 15.8 %copy-start.2 = (bf16[24,16,16,128]{3,2,1,0:T(8,128)(2,1)S(1)}, bf16[24,16,16,128]{3,2,1,0:T(8,128)(2,1)}, u32[]{:S(2)}) copy-start(bf16[24,16,16,128]{3,2,1,0:T(8,128)(2,1)} %param.12) | copy-start | bytes 4718596
  4.5 94.0 %all-to-all-start = ((bf16[4,16,16,128]{3,2,1,0:T(8,128)(2,1)}), bf16[4,16,16,128]{3,2,1,0:T(8,128)(2,1)}, u32[]{:S(2)}, u32[]{:S(2)}) async-start(bf16[4,16,16,128]{3,2,1,0:T(8,128)(2,1)} %broadcast_in_dim.36), calls=%async_computation | async-start | bytes 524288 | tf_op jit(solution)/shard_map/all_to_all | solution.py:44
  10.4 309.9 %collective-permute-start = (bf16[24,2,16,128]{3,2,1,0:T(8,128)(2,1)}, bf16[24,2,16,128]{3,2,1,0:T(8,128)(2,1)}, u32[]{:S(2)}, u32[]{:S(2)}) collective-permute-start(bf16[24,2,16,128]{3,2,1,0:T(8,128)(2,1)} %get-tuple-element.195), channel_id=1, source_target_pairs={{1,0},{2,1},{3,2},{4,3},{5,4},{6,5},{7,6},{8,7},{9,8},{10,9},{11,1... | collective-permute-start | bytes 589832 | tf_op jit(solution)/shard_map/ppermute | solution.py:29
  16.4 302.1 %collective-permute-start.1 = (bf16[24,2,16,128]{3,2,1,0:T(8,128)(2,1)}, bf16[24,2,16,128]{3,2,1,0:T(8,128)(2,1)}, u32[]{:S(2)}, u32[]{:S(2)}) collective-permute-start(bf16[24,2,16,128]{3,2,1,0:T(8,128)(2,1)} %get-tuple-element.196), channel_id=1, source_target_pairs={{0,1},{1,2},{2,3},{3,4},{4,5},{5,6},{6,7},{7,8},{8,9},{9,10},{10,1... | collective-permute-start | bytes 589832 | tf_op jit(solution)/shard_map/ppermute | solution.py:27
  17.5 82.1 %collective-permute-start.2 = (bf16[24,16,16,128]{3,0,2,1:T(8,128)(2,1)S(1)}, bf16[24,16,16,128]{3,0,2,1:T(8,128)(2,1)}, u32[]{:S(2)}, u32[]{:S(2)}) collective-permute-start(bf16[24,16,16,128]{3,0,2,1:T(8,128)(2,1)S(1)} %copy.15), channel_id=1, source_target_pairs={{1,0},{2,1},{3,2},{4,3},{5,4},{6,5},{7,6},{8,7},{9,8},{10,9},{11,1... | collective-permute-start | bytes 4718600 | tf_op jit(solution)/shard_map/ppermute | solution.py:39
  34.0 3.6 copy-start.11
  99.5 3.4 copy-start.12
  109.4 1.9 copy-start.4
  118.5 1.9 copy-start.4
  127.5 1.9 copy-start.4
  136.6 1.9 copy-start.4
  145.7 1.9 copy-start.4
  154.7 1.9 copy-start.4
  163.8 1.9 copy-start.4
  172.9 1.9 copy-start.4
  185.9 5.9 %slice-start = ((s8[6291456]{0:T(1024)(128)(4,1)}), s8[4194304]{0:T(1024)(128)(4,1)S(1)}, s32[]{:S(2)}) async-start(s8[6291456]{0:T(1024)(128)(4,1)} %bitcast.137), calls=%async_computation.1 | async-start | bytes 8388608 | tf_op jit(solution)/shard_map/while
  187.0 4.8 %slice-start.1 = ((s8[6291456]{0:T(1024)(128)(4,1)}), s8[2097152]{0:T(1024)(128)(4,1)S(1)}, s32[]{:S(2)}) async-start(s8[6291456]{0:T(1024)(128)(4,1)} %bitcast.137), calls=%async_computation.2 | async-start | bytes 4194304 | tf_op jit(solution)/shard_map/while
  192.9 2.6 copy-start.3
  202.5 5.9 %slice-start = ((s8[6291456]{0:T(1024)(128)(4,1)}), s8[4194304]{0:T(1024)(128)(4,1)S(1)}, s32[]{:S(2)}) async-start(s8[6291456]{0:T(1024)(128)(4,1)} %bitcast.137), calls=%async_computation.1 | async-start | bytes 8388608 | tf_op jit(solution)/shard_map/while
  203.5 4.8 %slice-start.1 = ((s8[6291456]{0:T(1024)(128)(4,1)}), s8[2097152]{0:T(1024)(128)(4,1)S(1)}, s32[]{:S(2)}) async-start(s8[6291456]{0:T(1024)(128)(4,1)} %bitcast.137), calls=%async_computation.2 | async-start | bytes 4194304 | tf_op jit(solution)/shard_map/while
  209.5 2.6 copy-start.3
  219.1 5.9 %slice-start = ((s8[6291456]{0:T(1024)(128)(4,1)}), s8[4194304]{0:T(1024)(128)(4,1)S(1)}, s32[]{:S(2)}) async-start(s8[6291456]{0:T(1024)(128)(4,1)} %bitcast.137), calls=%async_computation.1 | async-start | bytes 8388608 | tf_op jit(solution)/shard_map/while
  220.1 4.8 %slice-start.1 = ((s8[6291456]{0:T(1024)(128)(4,1)}), s8[2097152]{0:T(1024)(128)(4,1)S(1)}, s32[]{:S(2)}) async-start(s8[6291456]{0:T(1024)(128)(4,1)} %bitcast.137), calls=%async_computation.2 | async-start | bytes 4194304 | tf_op jit(solution)/shard_map/while
  226.1 2.6 copy-start.3
  235.7 5.9 %slice-start = ((s8[6291456]{0:T(1024)(128)(4,1)}), s8[4194304]{0:T(1024)(128)(4,1)S(1)}, s32[]{:S(2)}) async-start(s8[6291456]{0:T(1024)(128)(4,1)} %bitcast.137), calls=%async_computation.1 | async-start | bytes 8388608 | tf_op jit(solution)/shard_map/while
  236.7 4.8 %slice-start.1 = ((s8[6291456]{0:T(1024)(128)(4,1)}), s8[2097152]{0:T(1024)(128)(4,1)S(1)}, s32[]{:S(2)}) async-start(s8[6291456]{0:T(1024)(128)(4,1)} %bitcast.137), calls=%async_computation.2 | async-start | bytes 4194304 | tf_op jit(solution)/shard_map/while
  242.7 2.6 copy-start.3
  252.3 5.9 %slice-start = ((s8[6291456]{0:T(1024)(128)(4,1)}), s8[4194304]{0:T(1024)(128)(4,1)S(1)}, s32[]{:S(2)}) async-start(s8[6291456]{0:T(1024)(128)(4,1)} %bitcast.137), calls=%async_computation.1 | async-start | bytes 8388608 | tf_op jit(solution)/shard_map/while
  253.3 4.8 %slice-start.1 = ((s8[6291456]{0:T(1024)(128)(4,1)}), s8[2097152]{0:T(1024)(128)(4,1)S(1)}, s32[]{:S(2)}) async-start(s8[6291456]{0:T(1024)(128)(4,1)} %bitcast.137), calls=%async_computation.2 | async-start | bytes 4194304 | tf_op jit(solution)/shard_map/while
  259.3 2.6 copy-start.3
  268.9 5.9 %slice-start = ((s8[6291456]{0:T(1024)(128)(4,1)}), s8[4194304]{0:T(1024)(128)(4,1)S(1)}, s32[]{:S(2)}) async-start(s8[6291456]{0:T(1024)(128)(4,1)} %bitcast.137), calls=%async_computation.1 | async-start | bytes 8388608 | tf_op jit(solution)/shard_map/while
  269.9 4.8 %slice-start.1 = ((s8[6291456]{0:T(1024)(128)(4,1)}), s8[2097152]{0:T(1024)(128)(4,1)S(1)}, s32[]{:S(2)}) async-start(s8[6291456]{0:T(1024)(128)(4,1)} %bitcast.137), calls=%async_computation.2 | async-start | bytes 4194304 | tf_op jit(solution)/shard_map/while
  275.9 2.6 copy-start.3
  285.4 5.9 %slice-start = ((s8[6291456]{0:T(1024)(128)(4,1)}), s8[4194304]{0:T(1024)(128)(4,1)S(1)}, s32[]{:S(2)}) async-start(s8[6291456]{0:T(1024)(128)(4,1)} %bitcast.137), calls=%async_computation.1 | async-start | bytes 8388608 | tf_op jit(solution)/shard_map/while
  286.5 4.8 %slice-start.1 = ((s8[6291456]{0:T(1024)(128)(4,1)}), s8[2097152]{0:T(1024)(128)(4,1)S(1)}, s32[]{:S(2)}) async-start(s8[6291456]{0:T(1024)(128)(4,1)} %bitcast.137), calls=%async_computation.2 | async-start | bytes 4194304 | tf_op jit(solution)/shard_map/while
  292.4 2.6 copy-start.3
  302.0 5.9 %slice-start = ((s8[6291456]{0:T(1024)(128)(4,1)}), s8[4194304]{0:T(1024)(128)(4,1)S(1)}, s32[]{:S(2)}) async-start(s8[6291456]{0:T(1024)(128)(4,1)} %bitcast.137), calls=%async_computation.1 | async-start | bytes 8388608 | tf_op jit(solution)/shard_map/while
  303.1 4.8 %slice-start.1 = ((s8[6291456]{0:T(1024)(128)(4,1)}), s8[2097152]{0:T(1024)(128)(4,1)S(1)}, s32[]{:S(2)}) async-start(s8[6291456]{0:T(1024)(128)(4,1)} %bitcast.137), calls=%async_computation.2 | async-start | bytes 4194304 | tf_op jit(solution)/shard_map/while
  309.0 2.6 copy-start.3
  311.7 72.8 %slice-start.2 = ((s8[6291456]{0:T(1024)(128)(4,1)}), s8[4194304]{0:T(1024)(128)(4,1)S(1)}, s32[]{:S(2)}) async-start(s8[6291456]{0:T(1024)(128)(4,1)} %bitcast.139), calls=%async_computation.3 | async-start | bytes 8388608
  314.0 68.7 %collective-permute-start.3 = (f32[24,16,16,128]{3,2,1,0:T(8,128)S(1)}, f32[24,16,16,128]{3,2,1,0:T(8,128)S(1)}, u32[]{:S(2)}, u32[]{:S(2)}) collective-permute-start(f32[24,16,16,128]{3,2,1,0:T(8,128)S(1)} %slice.247), channel_id=1, source_target_pairs={{63,0},{0,1},{1,2},{2,3},{3,4},{4,5},{5,6},{6,7},{7,8},{8,9},{9,10... | collective-permute-start | bytes 9437192 | tf_op jit(solution)/shard_map/ppermute | solution.py:39
  314.1 66.9 %collective-permute-start.4 = (bf16[2,2,16,128]{3,2,1,0:T(8,128)(2,1)S(1)}, bf16[2,2,16,128]{3,2,1,0:T(8,128)(2,1)S(1)}, u32[]{:S(2)}, u32[]{:S(2)}) collective-permute-start(bf16[2,2,16,128]{3,2,1,0:T(8,128)(2,1)S(1)} %get-tuple-element.231), channel_id=1, source_target_pairs={{0,1},{1,2},{2,3},{3,4},{4,5},{5,6},{6,7},{7,8},{8,9},{9,10},{10,1... | collective-permute-start | bytes 49160 | tf_op jit(solution)/shard_map/ppermute | solution.py:27
  314.9 66.1 %collective-permute-start.5 = (bf16[2,2,16,128]{3,2,1,0:T(8,128)(2,1)S(1)}, bf16[2,2,16,128]{3,2,1,0:T(8,128)(2,1)S(1)}, u32[]{:S(2)}, u32[]{:S(2)}) collective-permute-start(bf16[2,2,16,128]{3,2,1,0:T(8,128)(2,1)S(1)} %get-tuple-element.232), channel_id=1, source_target_pairs={{1,0},{2,1},{3,2},{4,3},{5,4},{6,5},{7,6},{8,7},{9,8},{10,9},{11,1... | collective-permute-start | bytes 49160 | tf_op jit(solution)/shard_map/ppermute | solution.py:29
  319.5 65.0 %slice-start.3 = ((s8[6291456]{0:T(1024)(128)(4,1)}), s8[2097152]{0:T(1024)(128)(4,1)S(1)}, s32[]{:S(2)}) async-start(s8[6291456]{0:T(1024)(128)(4,1)} %bitcast.139), calls=%async_computation.4 | async-start | bytes 4194304
  320.2 60.9 %copy-start.7 = (bf16[24,18,16,128]{3,2,1,0:T(8,128)(2,1)}, bf16[24,18,16,128]{3,2,1,0:T(8,128)(2,1)S(1)}, u32[]{:S(2)}) copy-start(bf16[24,18,16,128]{3,2,1,0:T(8,128)(2,1)S(1)} %get-tuple-element.198) | copy-start | bytes 5308420
  320.2 61.6 %copy-start.10 = (f32[16,16,128]{2,1,0:T(8,128)S(1)}, f32[16,16,128]{2,1,0:T(8,128)}, u32[]{:S(2)}) copy-start(f32[16,16,128]{2,1,0:T(8,128)} %param.15) | copy-start | bytes 393220
  381.1 3.4 copy-start.5
  381.1 3.6 copy-start.6
  381.1 3.6 copy-start.9
  382.7 1.8 copy-start.8
  384.7 15.8 %copy-start.1 = (f32[13,13]{1,0:T(8,128)S(1)}, f32[13,13]{1,0:T(8,128)}, u32[]{:S(2)}) copy-start(f32[13,13]{1,0:T(8,128)} %param.19) | copy-start | bytes 2032
where the time goes:
time: 408 us; the launch traced here: 401 us
  local copies, waits for them, and re-layouts  144 us (35%)
  waiting for transfers between devices  59.4 us (15%)
  blocking collectives  52.8 us (13%)
  matrix products  47.1 us (12%)
  other arithmetic  45 us (11%)
  loops' own time  32.3 us (8%)
  starting transfers between devices  18.8 us (5%)
    ppermute x2, waiting for transfers between devices, padded(): lax.ppermute(tail, axis, [(i, (i + 1) % count) for i in range(count)])  59.4 us
    psum x5, blocking collectives, by_axis(): array = lax.psum(array, axis)  52.8 us
    while x64, local copies, waits for them, and re-layouts  24.6 us
    slice x8, local copies, waits for them, and re-layouts, local(): jnp.roll(center, -distance, dimension)  22.6 us
    dynamic_slice x32, local copies, waits for them, and re-layouts, gather_coefficients(): return lax.map(per_atom, (beta_block, starts, row_start, col_start))  21.5 us
    dynamic_slice x8, local copies, waits for them, and re-layouts, add_atom(): current = lax.dynamic_slice_in_dim(summed, plane, width, 1)  19.6 us
    dot_general x8, matrix products, add_atom(): jnp.einsum('piyz,po->oiyz', placed, weighted[atom_index], preferred_eleme...  18.8 us
    another operation x1, loops' own time, deposit(): return lax.fori_loop(0, beta_block.shape[0], add_atom, buffer)  16.4 us
  transfers between devices with their start and end apart: 7, of which 1 were waited for; matrix products, arithmetic and copies ran while one was open for 47% of the time, Pallas kernels for 0%

commit v1 on v0

v1 whole, which is shorter than its diff:
```python
import functools
import math

import jax
import jax.numpy as jnp
import numpy as np
from jax import lax
from jax.experimental import pallas as pl
from jax.experimental.pallas import tpu as pltpu
from jax.sharding import PartitionSpec as P

SCREENING = 0.25
SWEEPS = 2
FOUR_PI = 4.0 * math.pi
ROWGROUP = 8
MESH = pl.DeviceIdType.MESH
F32 = jnp.float32
BF16 = jnp.bfloat16
SLOT = 16


def stencil_matrices(planes, rows, cols):
    def line(count, periodic):
        matrix = np.zeros((count, count), np.float32)
        for distance, weight in ((1, 16.0), (2, -1.0)):
            for sign in (-1, 1):
                for index in range(count):
                    other = index + sign * distance
                    if periodic:
                        other %= count
                    if 0 <= other < count:
                        matrix[index, other] += weight
        return matrix

    left = np.kron(line(planes, False), np.eye(rows)) + np.kron(np.eye(planes), line(rows, True))
    right = line(cols, True) - 90.0 * np.eye(cols)
    return left.astype(np.float32), right.astype(np.float32)


def kernel(
    dims,
    box_ref,
    occ_ref,
    coup_ref,
    orb_ref,
    vin_ref,
    ion_ref,
    har_ref,
    proj_ref,
    left_ref,
    right_ref,
    app_ref,
    pot_ref,
    pprev,
    halo,
    hhalo,
    rhalo,
    dens_f,
    dens_b,
    dens_in,
    rho,
    chg1,
    chg2,
    chg3,
    chg_in1,
    chg_in2,
    chg_in3,
    colmat,
    scat,
    local_part,
    gathered,
    mask3,
    shifts,
    spread,
    packed,
    part_own,
    part_prev,
    got_own,
    got_prev,
    couple,
    nlt,
    hone,
    s_proj,
    r_proj,
    s_fwd,
    r_fwd,
    s_halo,
    r_halo,
    s_hh,
    r_hh,
    s_dens,
    r_dens,
    s_c1,
    r_c1,
    s_c2,
    r_c2,
    s_c3,
    r_c3,
    s_rh,
    r_rh,
    s_part,
    r_part,
):
    n_band, n_space, group = dims
    orbs, planes, rows, cols = orb_ref.shape
    atoms, nproj, width, square = proj_ref.shape
    cells = planes * rows
    n_far = n_space // group
    half = atoms // 2
    quarter = half // 2

    me_b = lax.axis_index("band")
    me_s = lax.axis_index("space")
    nxt = lax.rem(me_s + 1, n_space)
    prv = lax.rem(me_s + n_space - 1, n_space)
    core = lax.rem(me_b, 2)
    sib = me_b + 1 - 2 * core
    near = lax.rem(me_s, group)
    far = me_s // group

    def band_peer(d):
        return (lax.rem(me_b + d, n_band), me_s)

    def near_peer(d):
        return (me_b, far * group + lax.rem(near + d, group))

    def far_peer(d):
        return (me_b, lax.rem(far + d, n_far) * group + near)

    partners = [(me_b, nxt), (me_b, prv)]
    partners += [band_peer(d) for d in range(1, n_band)]
    partners += [near_peer(d) for d in range(1, group)]
    partners += [far_peer(d) for d in range(1, n_far)]
    barrier = pltpu.get_barrier_semaphore()
    for partner in partners:
        pl.semaphore_signal(barrier, inc=1, device_id=partner, device_id_type=MESH)
    pl.semaphore_wait(barrier, len(partners))

    sent = []

    def send(src, dst, send_sem, recv_sem, device):
        copy = pltpu.make_async_remote_copy(
            src_ref=src,
            dst_ref=dst,
            send_sem=send_sem,
            recv_sem=recv_sem,
            device_id=device,
            device_id_type=MESH,
        )
        copy.start()
        sent.append(copy)

    def arrived(dst, send_sem, recv_sem):
        pltpu.make_async_remote_copy(
            src_ref=dst,
            dst_ref=dst,
            send_sem=send_sem,
            recv_sem=recv_sem,
            device_id=(me_b, nxt),
            device_id_type=MESH,
        ).wait_recv()

    for h in range(2):
        some = pl.ds(core * half + h * quarter, quarter)
        send(proj_ref.at[some], pprev.at[some], s_proj.at[h], r_proj.at[h], (me_b, nxt))
    send(orb_ref.at[:, pl.ds(0, 2)], halo.at[1], s_halo.at[1], r_halo.at[1], (me_b, prv))
    send(har_ref.at[pl.ds(0, 2)], hhalo.at[1], s_hh.at[1], r_hh.at[1], (me_b, prv))
    send(har_ref.at[pl.ds(planes - 2, 2)], hhalo.at[0], s_hh.at[0], r_hh.at[0], (me_b, nxt))
    send(orb_ref.at[:, pl.ds(planes - 2, 2)], halo.at[0], s_halo.at[0], r_halo.at[0], (me_b, nxt))

    def density_plane(i, charge):
        total = jnp.zeros((rows, cols), F32)
        for o in range(orbs):
            field = orb_ref[o, i].astype(F32)
            total = total + (occ_ref[o] * field) * field
        dens_f[i] = total
        dens_b[i] = total.astype(BF16)
        for r in range(0, rows, ROWGROUP):
            charge = charge + total[r : r + ROWGROUP]
        return charge

    chg1[...] = lax.fori_loop(0, planes, density_plane, jnp.zeros((ROWGROUP, cols), F32))
    for d in range(1, n_band):
        send(dens_b, dens_in.at[me_b], s_dens.at[d], r_dens.at[me_b], band_peer(d))
        send(chg1, chg_in1.at[me_b], s_c1.at[d], r_c1.at[me_b], band_peer(d))

    def lane_table(first, which):
        lane = lax.broadcasted_iota(jnp.int32, (1, cols), 1)
        table = lax.rem(lane, SLOT)
        for a in range(atoms):
            table = table + jnp.where(lane // SLOT == a, box_ref[which, first + a], 0)
        return table

    first_own = me_s * atoms
    first_prev = prv * atoms
    colmat[:, 0:cols] = right_ref[...]
    zrow = lax.broadcasted_iota(jnp.int32, (cols, cols), 0)
    for part, first in ((0, first_own), (1, first_prev)):
        hot = jnp.where(zrow == lane_table(first, 2), 1.0, 0.0).astype(F32)
        colmat[:, (1 + part) * cols : (2 + part) * cols] = hot.astype(BF16)
        scat[part * cols : (part + 1) * cols, :] = hot.T.astype(BF16)

    def stencil(o, carry):
        field = orb_ref[o].reshape(cells, cols)
        summed = jnp.dot(left_ref[...], field, preferred_element_type=F32)
        wide = jnp.dot(field, colmat[...], preferred_element_type=F32)
        lap = summed + wide[:, 0:cols]
        local_part[o] = lap * (-0.5 / 12.0) + vin_ref[...].reshape(cells, cols) * field.astype(F32)
        gathered[0, pl.ds(o, cells, stride=orbs), :] = wide[:, cols : 2 * cols]
        gathered[1, pl.ds(o, cells, stride=orbs), :] = wide[:, 2 * cols : 3 * cols]
        return carry

    lax.fori_loop(0, orbs, stencil, 0)

    for d in range(1, n_band):
        peer = lax.rem(me_b + d, n_band)
        arrived(chg_in1.at[peer], s_c1.at[d], r_c1.at[peer])
    charge = chg1[...]
    for d in range(1, n_band):
        charge = charge + chg_in1[lax.rem(me_b + d, n_band)]
    chg2[...] = charge
    for d in range(1, group):
        send(chg2, chg_in2.at[near], s_c2.at[d], r_c2.at[near], near_peer(d))
    for d in range(1, n_band):
        peer = lax.rem(me_b + d, n_band)
        arrived(dens_in.at[peer], s_dens.at[d], r_dens.at[peer])
    total_density = dens_f[...]
    for d in range(1, n_band):
        total_density = total_density + dens_in[lax.rem(me_b + d, n_band)].astype(F32)
    rho[...] = total_density
    send(rho.at[0], rhalo.at[1], s_rh.at[1], r_rh.at[1], (me_b, prv))
    send(rho.at[planes - 1], rhalo.at[0], s_rh.at[0], r_rh.at[0], (me_b, nxt))

    spot = lax.broadcasted_iota(jnp.int32, (atoms, SLOT, cols), 2) // SLOT
    mask3[...] = jnp.where(
        spot == lax.broadcasted_iota(jnp.int32, (atoms, SLOT, cols), 0), 1.0, 0.0
    ).astype(BF16)
    r_idx = lax.broadcasted_iota(jnp.int32, (cells, nproj * width), 0)
    c_idx = lax.broadcasted_iota(jnp.int32, (cells, nproj * width), 1)
    shifts[...] = jnp.where(
        r_idx % SLOT == c_idx // width, r_idx // SLOT - c_idx % width, 4 * planes
    )

    def pack(part, source, first):
        for a in range(atoms):
            plane = lax.rem(box_ref[0, first + a], planes) - part * planes
            place = jnp.where(shifts[...] == plane, 1.0, 0.0).astype(BF16)
            spread[a] = jnp.dot(
                place, source[a].reshape(nproj * width, square), preferred_element_type=F32
            )

        slot = lax.broadcasted_iota(jnp.int32, (SLOT, cols), 1) // SLOT

        def turn(i, carry):
            at = pl.ds(pl.multiple_of(i * SLOT, SLOT), SLOT)
            for h in range(square // cols):
                x = [spread[a, at, h * cols : (h + 1) * cols] for a in range(atoms)]
                for d in (4, 2, 1):
                    low = (slot & d) == 0
                    for a in range(atoms):
                        if a & d:
                            continue
                        lo, hi = x[a], x[a + d]
                        x[a] = jnp.where(low, lo, pltpu.roll(hi, d * SLOT, 1))
                        x[a + d] = jnp.where(low, pltpu.roll(lo, cols - d * SLOT, 1), hi)
                for y in range(atoms):
                    packed[part, h * atoms + y, i] = x[y].astype(BF16)
            return carry

        lax.fori_loop(0, planes, turn, 0)

    def block(part, y, i):
        tile = packed[part, y, i]
        return (tile[None] * mask3[...]).reshape(atoms * SLOT, cols)

    def gather(part):
        def one(i, total):
            for y in range(0, rows, 2):
                base = pl.multiple_of((i * rows + y) * orbs, 8)
                boxes = jnp.concatenate(
                    [
                        gathered[part, pl.ds(base, orbs), :],
                        gathered[part, pl.ds(base + orbs, orbs), :],
                    ],
                    axis=1,
                ).astype(BF16)
                weights = jnp.concatenate([block(part, y, i), block(part, y + 1, i)], axis=1)
                total = total + lax.dot_general(
                    boxes, weights, (((1,), (1,)), ((), ())), preferred_element_type=F32
                )
            return total

        return lax.fori_loop(0, planes, one, jnp.zeros((orbs, atoms * SLOT), F32))

    pack(0, proj_ref, first_own)
    part_own[...] = gather(0)
    send(part_own, got_prev, s_part.at[0], r_part.at[0], (me_b, nxt))

    for d in range(1, group):
        peer = lax.rem(near + d, group)
        arrived(chg_in2.at[peer], s_c2.at[d], r_c2.at[peer])
    charge = chg2[...]
    for d in range(1, group):
        charge = charge + chg_in2[lax.rem(near + d, group)]
    chg3[...] = charge
    for d in range(1, n_far):
        send(chg3, chg_in3.at[far], s_c3.at[d], r_c3.at[far], far_peer(d))

    for h in range(2):
        some = pl.ds(core * half + h * quarter, quarter)
        arrived(pprev.at[some], s_proj.at[h], r_proj.at[h])
        send(pprev.at[some], pprev.at[some], s_fwd.at[h], r_fwd.at[h], (sib, me_s))
    for h in range(2):
        some = pl.ds((1 - core) * half + h * quarter, quarter)
        arrived(pprev.at[some], s_fwd.at[h], r_fwd.at[h])
    pack(1, pprev, first_prev)
    part_prev[...] = gather(1)
    send(part_prev, got_own, s_part.at[1], r_part.at[1], (me_b, prv))

    for side in range(2):
        arrived(hhalo.at[side], s_hh.at[side], r_hh.at[side])
        arrived(rhalo.at[side], s_rh.at[side], r_rh.at[side])

    def around(cell):
        return (
            pltpu.roll(cell, 1, 0)
            + pltpu.roll(cell, rows - 1, 0)
            + pltpu.roll(cell, 1, 1)
            + pltpu.roll(cell, cols - 1, 1)
        )

    def start_plane(p):
        if p < 0:
            return hhalo[0, p + 2]
        if p >= planes:
            return hhalo[1, p - planes]
        return har_ref[p]

    def rho_plane(p):
        if p < 0:
            return rhalo[0]
        if p >= planes:
            return rhalo[1]
        return rho[p]

    inverse = 1.0 / (6.0 + SCREENING)
    for p in range(-1, planes + 1):
        total = start_plane(p - 1) + start_plane(p + 1) + around(start_plane(p))
        hone[p + 1] = (total + FOUR_PI * rho_plane(p)) * inverse
    for d in range(1, n_far):
        peer = lax.rem(far + d, n_far)
        arrived(chg_in3.at[peer], s_c3.at[d], r_c3.at[peer])
    charge = chg3[...]
    for d in range(1, n_far):
        charge = charge + chg_in3[lax.rem(far + d, n_far)]
    mean = jnp.sum(charge, axis=(0, 1), keepdims=True) * (1.0 / (cells * cols * n_space))
    lift = FOUR_PI * inverse * (1.0 + 6.0 * inverse) * mean
    for p in range(planes):
        total = hone[p] + hone[p + 2] + around(hone[p + 1])
        second = (total + FOUR_PI * rho[p]) * inverse
        root = jnp.exp(jnp.log(rho[p] * (3.0 / math.pi)) * (1.0 / 3.0))
        pot_ref[p] = ion_ref[p] + (second - lift) - root

    for side in range(2):
        arrived(halo.at[side], s_halo.at[side], r_halo.at[side])

    def edges(o, carry):
        near_low, far_low = halo[0, o, 1].astype(F32), halo[0, o, 0].astype(F32)
        near_up, far_up = halo[1, o, 0].astype(F32), halo[1, o, 1].astype(F32)
        scale = -0.5 / 12.0
        last = cells - rows
        local_part[o, 0:rows] += scale * (16.0 * near_low - far_low)
        local_part[o, rows : 2 * rows] += (-scale) * near_low
        local_part[o, last : last + rows] += scale * (16.0 * near_up - far_up)
        local_part[o, last - rows : last] += (-scale) * near_up
        return carry

    lax.fori_loop(0, orbs, edges, 0)

    row_id = lax.broadcasted_iota(jnp.int32, (atoms * SLOT, nproj), 0) % SLOT
    pick = jnp.where(
        row_id == lax.broadcasted_iota(jnp.int32, (atoms * SLOT, nproj), 1), 1.0, 0.0
    ).astype(F32)
    contract = (((1,), (1,)), ((), ()))
    tall = lax.dot_general(
        pick, coup_ref[...], contract, precision=lax.Precision.HIGHEST, preferred_element_type=F32
    )
    full = lax.dot_general(
        tall, pick, contract, precision=lax.Precision.HIGHEST, preferred_element_type=F32
    )
    size = (atoms * SLOT, atoms * SLOT)
    same = (
        lax.broadcasted_iota(jnp.int32, size, 0) // SLOT
        == lax.broadcasted_iota(jnp.int32, size, 1) // SLOT
    )
    couple[...] = jnp.where(same, full, 0.0)

    arrived(got_prev, s_part.at[0], r_part.at[0])
    arrived(got_own, s_part.at[1], r_part.at[1])
    weighted = []
    for mine, other in ((part_own, got_own), (part_prev, got_prev)):
        weighted.append(
            jnp.dot(
                mine[...] + other[...],
                couple[...],
                precision=lax.Precision.HIGHEST,
                preferred_element_type=F32,
            ).astype(BF16)
        )

    def deposit(i, carry):
        spreads = []
        for part in range(2):
            terms = [
                jnp.dot(weighted[part], block(part, y, i), preferred_element_type=F32)
                for y in range(rows)
            ]
            spreads.append(jnp.concatenate(terms, axis=0).astype(BF16))
        nlt[...] = jnp.dot(
            jnp.concatenate(spreads, axis=1), scat[...], preferred_element_type=F32
        )
        at = pl.ds(pl.multiple_of(i * rows, rows), rows)
        for o in range(orbs):
            total = local_part[o, at, :] + nlt[pl.ds(o, rows, stride=orbs), :]
            app_ref[o, i] = total.astype(BF16)
        return carry

    lax.fori_loop(0, planes, deposit, 0)

    for copy in sent:
        copy.wait_send()


def local(
    n_band,
    n_space,
    orbitals,
    occupations,
    potential_in,
    ionic_potential,
    hartree_prev,
    projectors,
    box_start,
    coupling,
):
    orbs, planes, rows, cols = orbitals.shape
    atoms, nproj, width, square = projectors.shape
    cells = planes * rows
    group = 8 if n_space % 8 == 0 else 2
    n_far = n_space // group
    left, right = stencil_matrices(planes, rows, cols)
    packed_rows = atoms * SLOT
    vmem = pl.BlockSpec(memory_space=pltpu.VMEM)
    smem = pl.BlockSpec(memory_space=pltpu.SMEM)
    dma = pltpu.SemaphoreType.DMA
    scratch = [
        pltpu.VMEM(projectors.shape, BF16),
        pltpu.VMEM((2, orbs, 2, rows, cols), BF16),
        pltpu.VMEM((2, 2, rows, cols), F32),
        pltpu.VMEM((2, rows, cols), F32),
        pltpu.VMEM((planes, rows, cols), F32),
        pltpu.VMEM((planes, rows, cols), BF16),
        pltpu.VMEM((n_band, planes, rows, cols), BF16),
        pltpu.VMEM((planes, rows, cols), F32),
        pltpu.VMEM((ROWGROUP, cols), F32),
        pltpu.VMEM((ROWGROUP, cols), F32),
        pltpu.VMEM((ROWGROUP, cols), F32),
        pltpu.VMEM((n_band, ROWGROUP, cols), F32),
        pltpu.VMEM((group, ROWGROUP, cols), F32),
        pltpu.VMEM((n_far, ROWGROUP, cols), F32),
        pltpu.VMEM((cols, 3 * cols), BF16),
        pltpu.VMEM((2 * cols, cols), BF16),
        pltpu.VMEM((orbs, cells, cols), F32),
        pltpu.VMEM((2, cells * orbs, cols), F32),
        pltpu.VMEM((atoms, SLOT, cols), BF16),
        pltpu.VMEM((cells, nproj * width), jnp.int32),
        pltpu.VMEM((atoms, cells, square), F32),
        pltpu.VMEM((2, rows, planes, SLOT, cols), BF16),
        pltpu.VMEM((orbs, packed_rows), F32),
        pltpu.VMEM((orbs, packed_rows), F32),
        pltpu.VMEM((orbs, packed_rows), F32),
        pltpu.VMEM((orbs, packed_rows), F32),
        pltpu.VMEM((packed_rows, packed_rows), F32),
        pltpu.VMEM((rows * orbs, cols), F32),
        pltpu.VMEM((planes + 2, rows, cols), F32),
        dma((2,)),
        dma((2,)),
        dma((2,)),
        dma((2,)),
        dma((2,)),
        dma((2,)),
        dma((2,)),
        dma((2,)),
        dma((n_band,)),
        dma((n_band,)),
        dma((n_band,)),
        dma((n_band,)),
        dma((group,)),
        dma((group,)),
        dma((n_far,)),
        dma((n_far,)),
        dma((2,)),
        dma((2,)),
        dma((2,)),
        dma((2,)),
    ]
    return pl.pallas_call(
        functools.partial(kernel, (n_band, n_space, group)),
        out_shape=(
            jax.ShapeDtypeStruct(orbitals.shape, BF16),
            jax.ShapeDtypeStruct(potential_in.shape, F32),
        ),
        in_specs=[smem, smem] + [vmem] * 8,
        out_specs=(vmem, vmem),
        scratch_shapes=scratch,
        compiler_params=pltpu.CompilerParams(
            collective_id=0, has_side_effects=True, vmem_limit_bytes=56 * 1024 * 1024
        ),
    )(
        box_start,
        occupations,
        coupling,
        orbitals,
        potential_in,
        ionic_potential,
        hartree_prev,
        projectors,
        jnp.asarray(left, BF16),
        jnp.asarray(right, BF16),
    )


def solution(mesh):
    return jax.shard_map(
        functools.partial(local, mesh.shape["band"], mesh.shape["space"]),
        mesh=mesh,
        in_specs=(
            P("band", "space", None, None),
            P("band"),
            P("space", None, None),
            P("space", None, None),
            P("space", None, None),
            P("space", None, None, None),
            P(),
            P(),
        ),
        out_specs=(P("band", "space", None, None), P("space", None, None)),
        check_vma=False,
    )
```

time: 408 us -> 64.3 us (0.16); the launches traced: 401 us -> 64.2 us
  local copies, waits for them, and re-layouts: 144 us -> 3.65 us
  Pallas kernels: 0 us -> 59.9 us
  waiting for transfers between devices: 59.4 us -> 0 us
  blocking collectives: 52.8 us -> 0 us
  matrix products: 47.1 us -> 0 us
  other arithmetic: 45 us -> 0 us
  loops' own time: 32.3 us -> 0 us
  starting transfers between devices: 18.8 us -> 0 us
    dynamic_slice x73 -> x0, local copies, waits for them, and re-layouts: 63.2 us -> none  [the longest x32 21.5 us: gather_coefficients(): return lax.map(per_atom, (beta_block, starts, row_start, col_start))]
    pallas_call x0 -> x1, Pallas kernels: none -> 59.9 us  [local(): pl.pallas_call(functools.partial(kernel, (n_band, n_space, group)), out_s...]
    ppermute x6 -> x0, waiting for transfers between devices: 59.4 us -> none  [the longest x2 59.4 us: padded(): lax.ppermute(tail, axis, [(i, (i + 1) % count) for i in range(count)])]
    psum x5 -> x0, blocking collectives: 52.8 us -> none  [by_axis(): array = lax.psum(array, axis)]
    dot_general x49 -> x0, matrix products: 47.1 us -> none  [the longest x8 18.8 us: add_atom(): jnp.einsum('piyz,po->oiyz', placed, weighted[atom_index], preferred_eleme...]
    another operation x2 -> x0, loops' own time: 32.3 us -> none  [the longest x1 16.4 us: deposit(): return lax.fori_loop(0, beta_block.shape[0], add_atom, buffer)]
    slice x19 -> x0, local copies, waits for them, and re-layouts: 27.3 us -> none  [the longest x8 22.6 us: local(): jnp.roll(center, -distance, dimension)]
    while x64 -> x0, local copies, waits for them, and re-layouts: 24.6 us -> none
  transfers between devices with their start and end apart: 7 -> 0, of which waited for: 1 -> 0; matrix products, arithmetic and copies ran while one was open for 47% -> 0% of each run, Pallas kernels for 0% -> 0%
where the time goes in v1:
time: 64.3 us; the launch traced here: 64.2 us
  Pallas kernels  59.9 us (93%)
  local copies, waits for them, and re-layouts  3.65 us (6%)
  between operations  0.65 us (1%)
    pallas_call x1, Pallas kernels, local(): pl.pallas_call(functools.partial(kernel, (n_band, n_space, group)), out_s...  59.9 us
    unnamed x4, local copies, waits for them, and re-layouts  3.65 us

profile of v1, /device:TPU:24, one launch (start us, length us, event | category | flops | bytes accessed | tf_op | source)
XLA Modules:
  0.0 64.2 jit_solution(8398879755369069624)
XLA Ops:
  0.6 59.9 %shard_map.113 = (bf16[24,16,16,128]{3,2,1,0:T(8,128)(2,1)}, f32[16,16,128]{2,1,0:T(8,128)}) custom-call(s32[3,512]{1,0:T(4,128)} %box_ref.1, f32[24]{0:T(128)} %occ_ref.1, f32[13,13]{1,0:T(8,128)} %coup_ref.1, bf16[24,16,16,128]{3,2,1,0:T(8,128)(2,1)} %orb_ref.1, f32[16,16,128]{2,1,0:T(8,128)} %vin_ref.1, f32[16,16,128]{2,1,0:T(8,128)} %ion_ref.1, ...), custom_call_target="tpu_custom_call" | custom-call | tf_op jit(solution)/shard_map/pallas_call | solution.py:507
  60.5 0.0 copy-start
  60.5 3.0 %copy.14 = bf16[24,16,16,128]{3,2,1,0:T(8,128)(2,1)} copy(bf16[24,16,16,128]{3,2,1,0:T(8,128)(2,1)} %get-tuple-element.4) | data formatting | bytes 3145728
  63.5 0.0 copy-done
  63.5 0.7 %copy.15 = f32[16,16,128]{2,1,0:T(8,128)} copy(f32[16,16,128]{2,1,0:T(8,128)S(1)} %copy-done) | data formatting | bytes 262144
Async XLA Ops:
  60.5 3.0 %copy-start = (f32[16,16,128]{2,1,0:T(8,128)S(1)}, f32[16,16,128]{2,1,0:T(8,128)}, u32[]{:S(2)}) copy-start(f32[16,16,128]{2,1,0:T(8,128)} %get-tuple-element.5) | copy-start | bytes 393220

commit v2 on v1

--- a/solution.py
+++ b/solution.py
@@ -33,7 +33,7 @@
         return matrix
 
     left = np.kron(line(planes, False), np.eye(rows)) + np.kron(np.eye(planes), line(rows, True))
-    right = line(cols, True) - 90.0 * np.eye(cols)
+    right = np.kron(np.eye(2), line(cols, True) - 90.0 * np.eye(cols))
     return left.astype(np.float32), right.astype(np.float32)
 
 
@@ -65,20 +65,19 @@
     chg_in1,
     chg_in2,
     chg_in3,
-    colmat,
     scat,
     local_part,
+    fields,
     gathered,
-    mask3,
-    shifts,
-    spread,
-    packed,
+    turned,
+    partial,
+    weights,
+    added,
     part_own,
     part_prev,
     got_own,
     got_prev,
     couple,
-    nlt,
     hone,
     s_proj,
     r_proj,
@@ -172,6 +171,8 @@
         total = jnp.zeros((rows, cols), F32)
         for o in range(orbs):
             field = orb_ref[o, i].astype(F32)
+            at = (o * planes + i) * rows
+            fields[pl.ds(pl.multiple_of(at, rows), rows), :] = field
             total = total + (occ_ref[o] * field) * field
         dens_f[i] = total
         dens_b[i] = total.astype(BF16)
@@ -184,33 +185,39 @@
         send(dens_b, dens_in.at[me_b], s_dens.at[d], r_dens.at[me_b], band_peer(d))
         send(chg1, chg_in1.at[me_b], s_c1.at[d], r_c1.at[me_b], band_peer(d))
 
-    def lane_table(first, which):
-        lane = lax.broadcasted_iota(jnp.int32, (1, cols), 1)
-        table = lax.rem(lane, SLOT)
-        for a in range(atoms):
-            table = table + jnp.where(lane // SLOT == a, box_ref[which, first + a], 0)
-        return table
-
     first_own = me_s * atoms
     first_prev = prv * atoms
-    colmat[:, 0:cols] = right_ref[...]
-    zrow = lax.broadcasted_iota(jnp.int32, (cols, cols), 0)
     for part, first in ((0, first_own), (1, first_prev)):
-        hot = jnp.where(zrow == lane_table(first, 2), 1.0, 0.0).astype(F32)
-        colmat[:, (1 + part) * cols : (2 + part) * cols] = hot.astype(BF16)
-        scat[part * cols : (part + 1) * cols, :] = hot.T.astype(BF16)
-
-    def stencil(o, carry):
-        field = orb_ref[o].reshape(cells, cols)
-        summed = jnp.dot(left_ref[...], field, preferred_element_type=F32)
-        wide = jnp.dot(field, colmat[...], preferred_element_type=F32)
-        lap = summed + wide[:, 0:cols]
-        local_part[o] = lap * (-0.5 / 12.0) + vin_ref[...].reshape(cells, cols) * field.astype(F32)
-        gathered[0, pl.ds(o, cells, stride=orbs), :] = wide[:, cols : 2 * cols]
-        gathered[1, pl.ds(o, cells, stride=orbs), :] = wide[:, 2 * cols : 3 * cols]
+        for a in range(atoms):
+            want = lax.broadcasted_iota(jnp.int32, (SLOT, cols), 0) + box_ref[2, first + a]
+            zcol = lax.broadcasted_iota(jnp.int32, (SLOT, cols), 1)
+            at = (part * atoms + a) * SLOT
+            scat[at : at + SLOT, :] = jnp.where(zcol == want, 1.0, 0.0).astype(BF16)
+
+    def stencil(pair, carry):
+        first, second = orb_ref[2 * pair], orb_ref[2 * pair + 1]
+        both = jnp.concatenate([first.reshape(cells, cols), second.reshape(cells, cols)], axis=1)
+        lap = jnp.dot(left_ref[...], both, preferred_element_type=F32)
+        lap = lap + jnp.dot(both, right_ref[...], preferred_element_type=F32)
+        vin = vin_ref[...].reshape(cells, cols)
+        for n in range(2):
+            field = both[:, n * cols : (n + 1) * cols].astype(F32)
+            local_part[2 * pair + n] = lap[:, n * cols : (n + 1) * cols] * (-0.5 / 12.0) + vin * field
         return carry
 
-    lax.fori_loop(0, orbs, stencil, 0)
+    lax.fori_loop(0, orbs // 2, stencil, 0)
+
+    def boxes(y, carry):
+        line = fields[pl.ds(y, orbs * planes, stride=rows), :].astype(BF16)
+        cut = lax.dot_general(
+            scat[...], line, (((1,), (1,)), ((), ())), preferred_element_type=F32
+        ).astype(BF16)
+        at = pl.ds(pl.multiple_of(y * SLOT, SLOT), SLOT)
+        for n in range(2 * atoms):
+            gathered[n, at, :] = cut[n * SLOT : (n + 1) * SLOT, :]
+        return carry
+
+    lax.fori_loop(0, rows, boxes, 0)
 
     for d in range(1, n_band):
         peer = lax.rem(me_b + d, n_band)
@@ -231,69 +238,51 @@
     send(rho.at[0], rhalo.at[1], s_rh.at[1], r_rh.at[1], (me_b, prv))
     send(rho.at[planes - 1], rhalo.at[0], s_rh.at[0], r_rh.at[0], (me_b, nxt))
 
-    spot = lax.broadcasted_iota(jnp.int32, (atoms, SLOT, cols), 2) // SLOT
-    mask3[...] = jnp.where(
-        spot == lax.broadcasted_iota(jnp.int32, (atoms, SLOT, cols), 0), 1.0, 0.0
+    wide = orbs * planes
+    belongs = jnp.where(
+        lax.broadcasted_iota(jnp.int32, (orbs, wide), 1) // planes
+        == lax.broadcasted_iota(jnp.int32, (orbs, wide), 0),
+        1.0,
+        0.0,
     ).astype(BF16)
-    r_idx = lax.broadcasted_iota(jnp.int32, (cells, nproj * width), 0)
-    c_idx = lax.broadcasted_iota(jnp.int32, (cells, nproj * width), 1)
-    shifts[...] = jnp.where(
-        r_idx % SLOT == c_idx // width, r_idx // SLOT - c_idx % width, 4 * planes
+    step = (
+        lax.broadcasted_iota(jnp.int32, (width, wide), 1) % planes
+        - lax.broadcasted_iota(jnp.int32, (width, wide), 0)
     )
 
-    def pack(part, source, first):
+    def on_plane(part, first, a):
+        return step == lax.rem(box_ref[0, first + a], planes) - part * planes
+
+    def gather(part, source, first):
         for a in range(atoms):
-            plane = lax.rem(box_ref[0, first + a], planes) - part * planes
-            place = jnp.where(shifts[...] == plane, 1.0, 0.0).astype(BF16)
-            spread[a] = jnp.dot(
-                place, source[a].reshape(nproj * width, square), preferred_element_type=F32
+            beta = source[a].reshape(nproj * width, square)
+            turned[part * atoms + a] = beta.T
+            pairs = jnp.dot(beta, gathered[part * atoms + a], preferred_element_type=F32)
+            pairs = jnp.where(
+                on_plane(part, first, a)[None], pairs.reshape(nproj, width, wide), 0.0
             )
-
-        slot = lax.broadcasted_iota(jnp.int32, (SLOT, cols), 1) // SLOT
-
-        def turn(i, carry):
-            at = pl.ds(pl.multiple_of(i * SLOT, SLOT), SLOT)
-            for h in range(square // cols):
-                x = [spread[a, at, h * cols : (h + 1) * cols] for a in range(atoms)]
-                for d in (4, 2, 1):
-                    low = (slot & d) == 0
-                    for a in range(atoms):
-                        if a & d:
-                            continue
-                        lo, hi = x[a], x[a + d]
-                        x[a] = jnp.where(low, lo, pltpu.roll(hi, d * SLOT, 1))
-                        x[a + d] = jnp.where(low, pltpu.roll(lo, cols - d * SLOT, 1), hi)
-                for y in range(atoms):
-                    packed[part, h * atoms + y, i] = x[y].astype(BF16)
-            return carry
-
-        lax.fori_loop(0, planes, turn, 0)
-
-    def block(part, y, i):
-        tile = packed[part, y, i]
-        return (tile[None] * mask3[...]).reshape(atoms * SLOT, cols)
-
-    def gather(part):
-        def one(i, total):
-            for y in range(0, rows, 2):
-                base = pl.multiple_of((i * rows + y) * orbs, 8)
-                boxes = jnp.concatenate(
-                    [
-                        gathered[part, pl.ds(base, orbs), :],
-                        gathered[part, pl.ds(base + orbs, orbs), :],
-                    ],
-                    axis=1,
-                ).astype(BF16)
-                weights = jnp.concatenate([block(part, y, i), block(part, y + 1, i)], axis=1)
-                total = total + lax.dot_general(
-                    boxes, weights, (((1,), (1,)), ((), ())), preferred_element_type=F32
-                )
-            return total
-
-        return lax.fori_loop(0, planes, one, jnp.zeros((orbs, atoms * SLOT), F32))
-
-    pack(0, proj_ref, first_own)
-    part_own[...] = gather(0)
+            folded = pairs[:, :ROWGROUP] + pairs[:, ROWGROUP:]
+            folded = folded.reshape(nproj * ROWGROUP, wide)
+            at = a * nproj * ROWGROUP
+            for t in range(wide // cols):
+                partial[t, at : at + nproj * ROWGROUP] = folded[:, t * cols : (t + 1) * cols]
+        count = atoms * nproj
+        tiles = []
+        for t in range(wide // cols):
+            total = partial[t, pl.ds(0, count, stride=ROWGROUP), :]
+            for r in range(1, ROWGROUP):
+                total = total + partial[t, pl.ds(r, count, stride=ROWGROUP), :]
+            tiles.append(total)
+        total = jnp.concatenate(tiles, axis=1)
+        total = jnp.concatenate([total, jnp.zeros((cols - count, wide), F32)], axis=0)
+        high = total.astype(BF16)
+        low = (total - high.astype(F32)).astype(BF16)
+        lanes = (((1,), (1,)), ((), ()))
+        return lax.dot_general(
+            belongs, high, lanes, preferred_element_type=F32
+        ) + lax.dot_general(belongs, low, lanes, preferred_element_type=F32)
+
+    part_own[...] = gather(0, proj_ref, first_own)
     send(part_own, got_prev, s_part.at[0], r_part.at[0], (me_b, nxt))
 
     for d in range(1, group):
@@ -313,8 +302,7 @@
     for h in range(2):
         some = pl.ds((1 - core) * half + h * quarter, quarter)
         arrived(pprev.at[some], s_fwd.at[h], r_fwd.at[h])
-    pack(1, pprev, first_prev)
-    part_prev[...] = gather(1)
+    part_prev[...] = gather(1, pprev, first_prev)
     send(part_prev, got_own, s_part.at[1], r_part.at[1], (me_b, prv))
 
     for side in range(2):
@@ -377,55 +365,66 @@
 
     lax.fori_loop(0, orbs, edges, 0)
 
-    row_id = lax.broadcasted_iota(jnp.int32, (atoms * SLOT, nproj), 0) % SLOT
+    row_id = lax.broadcasted_iota(jnp.int32, (cols, nproj), 0) % nproj
     pick = jnp.where(
-        row_id == lax.broadcasted_iota(jnp.int32, (atoms * SLOT, nproj), 1), 1.0, 0.0
+        row_id == lax.broadcasted_iota(jnp.int32, (cols, nproj), 1), 1.0, 0.0
     ).astype(F32)
-    contract = (((1,), (1,)), ((), ()))
-    tall = lax.dot_general(
-        pick, coup_ref[...], contract, precision=lax.Precision.HIGHEST, preferred_element_type=F32
+    tall = jnp.dot(
+        pick, coup_ref[...], precision=lax.Precision.HIGHEST, preferred_element_type=F32
     )
     full = lax.dot_general(
-        tall, pick, contract, precision=lax.Precision.HIGHEST, preferred_element_type=F32
+        tall,
+        pick,
+        (((1,), (1,)), ((), ())),
+        precision=lax.Precision.HIGHEST,
+        preferred_element_type=F32,
     )
-    size = (atoms * SLOT, atoms * SLOT)
     same = (
-        lax.broadcasted_iota(jnp.int32, size, 0) // SLOT
-        == lax.broadcasted_iota(jnp.int32, size, 1) // SLOT
+        lax.broadcasted_iota(jnp.int32, (cols, cols), 0) // nproj
+        == lax.broadcasted_iota(jnp.int32, (cols, cols), 1) // nproj
     )
     couple[...] = jnp.where(same, full, 0.0)
 
     arrived(got_prev, s_part.at[0], r_part.at[0])
     arrived(got_own, s_part.at[1], r_part.at[1])
-    weighted = []
-    for mine, other in ((part_own, got_own), (part_prev, got_prev)):
-        weighted.append(
-            jnp.dot(
-                mine[...] + other[...],
-                couple[...],
-                precision=lax.Precision.HIGHEST,
-                preferred_element_type=F32,
+    for part, mine, other, first in (
+        (0, part_own, got_own, first_own),
+        (1, part_prev, got_prev, first_prev),
+    ):
+        weighted = lax.dot_general(
+            couple[...],
+            mine[...] + other[...],
+            (((1,), (1,)), ((), ())),
+            precision=lax.Precision.HIGHEST,
+            preferred_element_type=F32,
+        ).astype(BF16)
+        weights[...] = jnp.dot(weighted, belongs, preferred_element_type=F32)
+        for a in range(atoms):
+            rows_a = weights[a * nproj : (a + 1) * nproj, :].reshape(nproj, 1, wide)
+            placed = jnp.where(on_plane(part, first, a)[None], rows_a, 0.0)
+            placed = placed.reshape(nproj * width, wide).astype(BF16)
+            term = jnp.dot(
+                turned[part * atoms + a], placed, preferred_element_type=F32
             ).astype(BF16)
+            at = (part * atoms + a) * SLOT
+            for y in range(rows):
+                added[y, at : at + SLOT, :] = term[y * SLOT : (y + 1) * SLOT, :]
+
+    def scatter(y, carry):
+        fields[pl.ds(y, wide, stride=rows), :] = lax.dot_general(
+            added[y], scat[...], (((0,), (0,)), ((), ())), preferred_element_type=F32
         )
-
-    def deposit(i, carry):
-        spreads = []
-        for part in range(2):
-            terms = [
-                jnp.dot(weighted[part], block(part, y, i), preferred_element_type=F32)
-                for y in range(rows)
-            ]
-            spreads.append(jnp.concatenate(terms, axis=0).astype(BF16))
-        nlt[...] = jnp.dot(
-            jnp.concatenate(spreads, axis=1), scat[...], preferred_element_type=F32
-        )
-        at = pl.ds(pl.multiple_of(i * rows, rows), rows)
-        for o in range(orbs):
-            total = local_part[o, at, :] + nlt[pl.ds(o, rows, stride=orbs), :]
-            app_ref[o, i] = total.astype(BF16)
         return carry
 
-    lax.fori_loop(0, planes, deposit, 0)
+    lax.fori_loop(0, rows, scatter, 0)
+
+    def finish(o, carry):
+        at = pl.ds(pl.multiple_of(o * cells, cells), cells)
+        total = local_part[o] + fields[at, :]
+        app_ref[o] = total.astype(BF16).reshape(planes, rows, cols)
+        return carry
+
+    lax.fori_loop(0, orbs, finish, 0)
 
     for copy in sent:
         copy.wait_send()
@@ -449,7 +448,6 @@
     group = 8 if n_space % 8 == 0 else 2
     n_far = n_space // group
     left, right = stencil_matrices(planes, rows, cols)
-    packed_rows = atoms * SLOT
     vmem = pl.BlockSpec(memory_space=pltpu.VMEM)
     smem = pl.BlockSpec(memory_space=pltpu.SMEM)
     dma = pltpu.SemaphoreType.DMA
@@ -468,20 +466,19 @@
         pltpu.VMEM((n_band, ROWGROUP, cols), F32),
         pltpu.VMEM((group, ROWGROUP, cols), F32),
         pltpu.VMEM((n_far, ROWGROUP, cols), F32),
-        pltpu.VMEM((cols, 3 * cols), BF16),
-        pltpu.VMEM((2 * cols, cols), BF16),
+        pltpu.VMEM((2 * atoms * SLOT, cols), BF16),
         pltpu.VMEM((orbs, cells, cols), F32),
-        pltpu.VMEM((2, cells * orbs, cols), F32),
-        pltpu.VMEM((atoms, SLOT, cols), BF16),
-        pltpu.VMEM((cells, nproj * width), jnp.int32),
-        pltpu.VMEM((atoms, cells, square), F32),
-        pltpu.VMEM((2, rows, planes, SLOT, cols), BF16),
-        pltpu.VMEM((orbs, packed_rows), F32),
-        pltpu.VMEM((orbs, packed_rows), F32),
-        pltpu.VMEM((orbs, packed_rows), F32),
-        pltpu.VMEM((orbs, packed_rows), F32),
-        pltpu.VMEM((packed_rows, packed_rows), F32),
-        pltpu.VMEM((rows * orbs, cols), F32),
+        pltpu.VMEM((orbs * cells, cols), F32),
+        pltpu.VMEM((2 * atoms, square, orbs * planes), BF16),
+        pltpu.VMEM((2 * atoms, square, nproj * width), BF16),
+        pltpu.VMEM((orbs * planes // cols, atoms * nproj * ROWGROUP, cols), F32),
+        pltpu.VMEM((cols, orbs * planes), F32),
+        pltpu.VMEM((rows, 2 * atoms * SLOT, orbs * planes), BF16),
+        pltpu.VMEM((orbs, cols), F32),
+        pltpu.VMEM((orbs, cols), F32),
+        pltpu.VMEM((orbs, cols), F32),
+        pltpu.VMEM((orbs, cols), F32),
+        pltpu.VMEM((cols, cols), F32),
         pltpu.VMEM((planes + 2, rows, cols), F32),
         dma((2,)),
         dma((2,)),

time: 64.3 us -> 50.8 us (0.79)
  the two profiles are of different devices: /device:TPU:24 before, /device:TPU:1 now
where the time goes in v2:
time: 50.8 us; the launch traced here: 50.7 us
  Pallas kernels  46.4 us (91%)
  local copies, waits for them, and re-layouts  3.65 us (7%)
  between operations  0.65 us (1%)
    pallas_call x1, Pallas kernels, local(): pl.pallas_call(functools.partial(kernel, (n_band, n_space, group)), out_s...  46.4 us
    unnamed x4, local copies, waits for them, and re-layouts  3.65 us

profile of v2, /device:TPU:1, one launch (start us, length us, event | category | flops | bytes accessed | tf_op | source)
XLA Modules:
  0.0 50.7 jit_solution(9762649451358317214)
XLA Ops:
  0.6 46.4 %shard_map.113 = (bf16[24,16,16,128]{3,2,1,0:T(8,128)(2,1)}, f32[16,16,128]{2,1,0:T(8,128)}) custom-call(s32[3,512]{1,0:T(4,128)} %box_ref.1, f32[24]{0:T(128)} %occ_ref.1, f32[13,13]{1,0:T(8,128)} %coup_ref.1, bf16[24,16,16,128]{3,2,1,0:T(8,128)(2,1)} %orb_ref.1, f32[16,16,128]{2,1,0:T(8,128)} %vin_ref.1, f32[16,16,128]{2,1,0:T(8,128)} %ion_ref.1, ...), custom_call_target="tpu_custom_call" | custom-call | tf_op jit(solution)/shard_map/pallas_call | solution.py:504
  47.0 0.0 copy-start
  47.0 3.0 %copy.14 = bf16[24,16,16,128]{3,2,1,0:T(8,128)(2,1)} copy(bf16[24,16,16,128]{3,2,1,0:T(8,128)(2,1)} %get-tuple-element.4) | data formatting | bytes 3145728
  50.0 0.0 copy-done
  50.0 0.7 %copy.15 = f32[16,16,128]{2,1,0:T(8,128)} copy(f32[16,16,128]{2,1,0:T(8,128)S(1)} %copy-done) | data formatting | bytes 262144
Async XLA Ops:
  47.0 3.0 %copy-start = (f32[16,16,128]{2,1,0:T(8,128)S(1)}, f32[16,16,128]{2,1,0:T(8,128)}, u32[]{:S(2)}) copy-start(f32[16,16,128]{2,1,0:T(8,128)} %get-tuple-element.5) | copy-start | bytes 393220

commit v3 on v2

v3 whole, which is shorter than its diff:
```python
import functools
import math

import jax
import jax.numpy as jnp
import numpy as np
from jax import lax
from jax.experimental import pallas as pl
from jax.experimental.pallas import tpu as pltpu
from jax.sharding import PartitionSpec as P

SCREENING = 0.25
SWEEPS = 2
FOUR_PI = 4.0 * math.pi
ROWGROUP = 8
MESH = pl.DeviceIdType.MESH
F32 = jnp.float32
BF16 = jnp.bfloat16
SLOT = 16


def stencil_matrices(planes, rows, cols):
    def line(count, periodic):
        matrix = np.zeros((count, count), np.float32)
        for distance, weight in ((1, 16.0), (2, -1.0)):
            for sign in (-1, 1):
                for index in range(count):
                    other = index + sign * distance
                    if periodic:
                        other %= count
                    if 0 <= other < count:
                        matrix[index, other] += weight
        return matrix

    left = np.kron(line(planes, False), np.eye(rows)) + np.kron(np.eye(planes), line(rows, True))
    right = np.kron(np.eye(2), line(cols, True) - 90.0 * np.eye(cols))
    return left.astype(np.float32), right.astype(np.float32)


def tables(box_ref, first_own, first_prev, scat, atoms, cols):
    for part, first in ((0, first_own), (1, first_prev)):
        for a in range(atoms):
            want = lax.broadcasted_iota(jnp.int32, (SLOT, cols), 0) + box_ref[2, first + a]
            zcol = lax.broadcasted_iota(jnp.int32, (SLOT, cols), 1)
            at = (part * atoms + a) * SLOT
            scat[at : at + SLOT, :] = jnp.where(zcol == want, 1.0, 0.0).astype(BF16)


def ownership(orbs, wide, planes):
    lane = lax.broadcasted_iota(jnp.int32, (orbs, wide), 1) // planes
    own = lane == lax.broadcasted_iota(jnp.int32, (orbs, wide), 0)
    return jnp.where(own, 1.0, 0.0).astype(BF16)


def plane_steps(width, wide, planes):
    lane = lax.broadcasted_iota(jnp.int32, (width, wide), 1) % planes
    return lane - lax.broadcasted_iota(jnp.int32, (width, wide), 0)


def exchange(
    dims,
    box_ref,
    occ_ref,
    coup_ref,
    orb_hbm,
    vin_hbm,
    har_hbm,
    proj_hbm,
    left_hbm,
    right_hbm,
    local_out,
    turned_out,
    halo,
    weighted_out,
    pre_ref,
    orb_ref,
    vin_ref,
    har_ref,
    proj_ref,
    left_ref,
    right_ref,
    pprev,
    hhalo,
    rhalo,
    dens_f,
    dens_b,
    dens_in,
    rho,
    chg1,
    chg2,
    chg3,
    chg_in1,
    chg_in2,
    chg_in3,
    scat,
    local_part,
    fields,
    gathered,
    turned,
    partial,
    part_own,
    part_prev,
    got_own,
    got_prev,
    couple,
    hone,
    s_load,
    s_store,
    s_proj,
    r_proj,
    s_fwd,
    r_fwd,
    s_halo,
    r_halo,
    s_hh,
    r_hh,
    s_dens,
    r_dens,
    s_c1,
    r_c1,
    s_c2,
    r_c2,
    s_c3,
    r_c3,
    s_rh,
    r_rh,
    s_part,
    r_part,
):
    n_band, n_space, group = dims
    orbs, planes, rows, cols = orb_ref.shape
    atoms, nproj, width, square = proj_ref.shape
    cells = planes * rows
    wide = orbs * planes
    n_far = n_space // group
    half = atoms // 2

    me_b = lax.axis_index("band")
    me_s = lax.axis_index("space")
    nxt = lax.rem(me_s + 1, n_space)
    prv = lax.rem(me_s + n_space - 1, n_space)
    core = lax.rem(me_b, 2)
    sib = me_b + 1 - 2 * core
    near = lax.rem(me_s, group)
    far = me_s // group

    def band_peer(d):
        return (lax.rem(me_b + d, n_band), me_s)

    def near_peer(d):
        return (me_b, far * group + lax.rem(near + d, group))

    def far_peer(d):
        return (me_b, lax.rem(far + d, n_far) * group + near)

    partners = [(me_b, nxt), (me_b, prv)]
    partners += [band_peer(d) for d in range(1, n_band)]
    partners += [near_peer(d) for d in range(1, group)]
    partners += [far_peer(d) for d in range(1, n_far)]
    barrier = pltpu.get_barrier_semaphore()
    for partner in partners:
        pl.semaphore_signal(barrier, inc=1, device_id=partner, device_id_type=MESH)

    loads = []
    for n, (src, dst) in enumerate(
        (
            (orb_hbm, orb_ref),
            (proj_hbm, proj_ref),
            (left_hbm, left_ref),
            (right_hbm, right_ref),
            (vin_hbm, vin_ref),
            (har_hbm, har_ref),
        )
    ):
        loads.append(pltpu.make_async_copy(src, dst, s_load.at[n]))
        loads[n].start()

    pl.semaphore_wait(barrier, len(partners))

    sent = []

    def send(src, dst, send_sem, recv_sem, device):
        copy = pltpu.make_async_remote_copy(
            src_ref=src,
            dst_ref=dst,
            send_sem=send_sem,
            recv_sem=recv_sem,
            device_id=device,
            device_id_type=MESH,
        )
        copy.start()
        sent.append(copy)

    def arrived(dst, send_sem, recv_sem):
        pltpu.make_async_remote_copy(
            src_ref=dst,
            dst_ref=dst,
            send_sem=send_sem,
            recv_sem=recv_sem,
            device_id=(me_b, nxt),
            device_id_type=MESH,
        ).wait_recv()

    for h in range(half):
        a = core * half + h
        send(proj_hbm.at[a], pprev.at[a], s_proj.at[h], r_proj.at[h], (me_b, nxt))
    send(har_hbm.at[pl.ds(0, 2)], hhalo.at[1], s_hh.at[1], r_hh.at[1], (me_b, prv))
    send(har_hbm.at[pl.ds(planes - 2, 2)], hhalo.at[0], s_hh.at[0], r_hh.at[0], (me_b, nxt))
    first_own = me_s * atoms
    first_prev = prv * atoms
    tables(box_ref, first_own, first_prev, scat, atoms, cols)

    loads[0].wait()

    def density_plane(i, charge):
        total = jnp.zeros((rows, cols), F32)
        for o in range(orbs):
            field = orb_ref[o, i].astype(F32)
            at = (o * planes + i) * rows
            fields[pl.ds(pl.multiple_of(at, rows), rows), :] = field
            total = total + (occ_ref[o] * field) * field
        dens_f[i] = total
        dens_b[i] = total.astype(BF16)
        for r in range(0, rows, ROWGROUP):
            charge = charge + total[r : r + ROWGROUP]
        return charge

    chg1[...] = lax.fori_loop(0, planes, density_plane, jnp.zeros((ROWGROUP, cols), F32))
    for d in range(1, n_band):
        send(chg1, chg_in1.at[me_b], s_c1.at[d], r_c1.at[me_b], band_peer(d))
    for d in range(1, n_band):
        send(dens_b, dens_in.at[me_b], s_dens.at[d], r_dens.at[me_b], band_peer(d))
    send(orb_ref.at[:, pl.ds(0, 2)], halo.at[1], s_halo.at[1], r_halo.at[1], (me_b, prv))
    send(orb_ref.at[:, pl.ds(planes - 2, 2)], halo.at[0], s_halo.at[0], r_halo.at[0], (me_b, nxt))

    for y in range(rows):
        line = fields[pl.ds(y, wide, stride=rows), :].astype(BF16)
        cut = lax.dot_general(
            scat[...], line, (((1,), (1,)), ((), ())), preferred_element_type=F32
        ).astype(BF16)
        for n in range(2 * atoms):
            gathered[n, y * SLOT : (y + 1) * SLOT, :] = cut[n * SLOT : (n + 1) * SLOT, :]

    for d in range(1, n_band):
        peer = lax.rem(me_b + d, n_band)
        arrived(chg_in1.at[peer], s_c1.at[d], r_c1.at[peer])
    charge = chg1[...]
    for d in range(1, n_band):
        charge = charge + chg_in1[lax.rem(me_b + d, n_band)]
    chg2[...] = charge
    for d in range(1, group):
        send(chg2, chg_in2.at[near], s_c2.at[d], r_c2.at[near], near_peer(d))

    belongs = ownership(orbs, wide, planes)
    step = plane_steps(width, wide, planes)

    def gather(part, source, first, a):
        beta = source[a].reshape(nproj * width, square)
        turned[part * atoms + a] = beta.T
        pairs = jnp.dot(beta, gathered[part * atoms + a], preferred_element_type=F32)
        keep = step == lax.rem(box_ref[0, first + a], planes) - part * planes
        pairs = jnp.where(keep[None], pairs.reshape(nproj, width, wide), 0.0)
        folded = pairs[:, :ROWGROUP] + pairs[:, ROWGROUP:]
        folded = folded.reshape(nproj * ROWGROUP, wide)
        at = pl.ds(pl.multiple_of(a * nproj * ROWGROUP, ROWGROUP), nproj * ROWGROUP)
        for t in range(wide // cols):
            partial[t, at, :] = folded[:, t * cols : (t + 1) * cols]

    def gathered_sum():
        count = atoms * nproj
        tiles = []
        for t in range(wide // cols):
            total = partial[t, pl.ds(0, count, stride=ROWGROUP), :]
            for r in range(1, ROWGROUP):
                total = total + partial[t, pl.ds(r, count, stride=ROWGROUP), :]
            tiles.append(total)
        total = jnp.concatenate(tiles, axis=1)
        total = jnp.concatenate([total, jnp.zeros((cols - count, wide), F32)], axis=0)
        high = total.astype(BF16)
        low = (total - high.astype(F32)).astype(BF16)
        lanes = (((1,), (1,)), ((), ()))
        return lax.dot_general(
            belongs, high, lanes, preferred_element_type=F32
        ) + lax.dot_general(belongs, low, lanes, preferred_element_type=F32)

    def hand_on(h):
        a = core * half + h
        arrived(pprev.at[a], s_proj.at[h], r_proj.at[h])
        send(pprev.at[a], pprev.at[a], s_fwd.at[h], r_fwd.at[h], (sib, me_s))

    loads[1].wait()
    for a in range(atoms):
        gather(0, proj_ref, first_own, a)
    part_own[...] = gathered_sum()
    send(part_own, got_prev, s_part.at[0], r_part.at[0], (me_b, nxt))

    hand_on(0)

    for n in range(2, 5):
        loads[n].wait()
    for pair in range(orbs // 2):
        first, second = orb_ref[2 * pair], orb_ref[2 * pair + 1]
        both = jnp.concatenate([first.reshape(cells, cols), second.reshape(cells, cols)], axis=1)
        lap = jnp.dot(left_ref[...], both, preferred_element_type=F32)
        lap = lap + jnp.dot(both, right_ref[...], preferred_element_type=F32)
        vin = vin_ref[...].reshape(cells, cols)
        for n in range(2):
            field = both[:, n * cols : (n + 1) * cols].astype(F32)
            local_part[2 * pair + n] = lap[:, n * cols : (n + 1) * cols] * (-0.5 / 12.0) + vin * field
    stores = [
        pltpu.make_async_copy(local_part, local_out, s_store.at[0]),
        pltpu.make_async_copy(
            turned.at[pl.ds(0, atoms)], turned_out.at[pl.ds(0, atoms)], s_store.at[1]
        ),
        pltpu.make_async_copy(
            turned.at[pl.ds(atoms, atoms)], turned_out.at[pl.ds(atoms, atoms)], s_store.at[2]
        ),
    ]
    stores[0].start()
    stores[1].start()

    hand_on(1)

    for d in range(1, n_band):
        peer = lax.rem(me_b + d, n_band)
        arrived(dens_in.at[peer], s_dens.at[d], r_dens.at[peer])
    total_density = dens_f[...]
    for d in range(1, n_band):
        total_density = total_density + dens_in[lax.rem(me_b + d, n_band)].astype(F32)
    rho[...] = total_density
    send(rho.at[0], rhalo.at[1], s_rh.at[1], r_rh.at[1], (me_b, prv))
    send(rho.at[planes - 1], rhalo.at[0], s_rh.at[0], r_rh.at[0], (me_b, nxt))
    for d in range(1, group):
        peer = lax.rem(near + d, group)
        arrived(chg_in2.at[peer], s_c2.at[d], r_c2.at[peer])
    charge = chg2[...]
    for d in range(1, group):
        charge = charge + chg_in2[lax.rem(near + d, group)]
    chg3[...] = charge
    for d in range(1, n_far):
        send(chg3, chg_in3.at[far], s_c3.at[d], r_c3.at[far], far_peer(d))

    for h in range(2, half):
        hand_on(h)
        gather(1, pprev, first_prev, core * half + h - 2)
    for h in range(half):
        a = (1 - core) * half + h
        arrived(pprev.at[a], s_fwd.at[h], r_fwd.at[h])
        gather(1, pprev, first_prev, a)
        if h < 2:
            gather(1, pprev, first_prev, core * half + half - 2 + h)
    part_prev[...] = gathered_sum()
    send(part_prev, got_own, s_part.at[1], r_part.at[1], (me_b, prv))
    stores[2].start()

    loads[5].wait()
    for side in range(2):
        arrived(hhalo.at[side], s_hh.at[side], r_hh.at[side])
        arrived(rhalo.at[side], s_rh.at[side], r_rh.at[side])

    def around(cell):
        return (
            pltpu.roll(cell, 1, 0)
            + pltpu.roll(cell, rows - 1, 0)
            + pltpu.roll(cell, 1, 1)
            + pltpu.roll(cell, cols - 1, 1)
        )

    def start_plane(p):
        if p < 0:
            return hhalo[0, p + 2]
        if p >= planes:
            return hhalo[1, p - planes]
        return har_ref[p]

    def rho_plane(p):
        if p < 0:
            return rhalo[0]
        if p >= planes:
            return rhalo[1]
        return rho[p]

    inverse = 1.0 / (6.0 + SCREENING)
    for p in range(-1, planes + 1):
        total = start_plane(p - 1) + start_plane(p + 1) + around(start_plane(p))
        hone[p + 1] = (total + FOUR_PI * rho_plane(p)) * inverse
    for d in range(1, n_far):
        peer = lax.rem(far + d, n_far)
        arrived(chg_in3.at[peer], s_c3.at[d], r_c3.at[peer])
    charge = chg3[...]
    for d in range(1, n_far):
        charge = charge + chg_in3[lax.rem(far + d, n_far)]
    mean = jnp.sum(charge, axis=(0, 1), keepdims=True) * (1.0 / (cells * cols * n_space))
    lift = FOUR_PI * inverse * (1.0 + 6.0 * inverse) * mean
    for p in range(planes):
        total = hone[p] + hone[p + 2] + around(hone[p + 1])
        second = (total + FOUR_PI * rho[p]) * inverse
        root = jnp.exp(jnp.log(rho[p] * (3.0 / math.pi)) * (1.0 / 3.0))
        pre_ref[p] = (second - lift) - root

    row_id = lax.broadcasted_iota(jnp.int32, (cols, nproj), 0) % nproj
    pick = jnp.where(
        row_id == lax.broadcasted_iota(jnp.int32, (cols, nproj), 1), 1.0, 0.0
    ).astype(F32)
    tall = jnp.dot(
        pick, coup_ref[...], precision=lax.Precision.HIGHEST, preferred_element_type=F32
    )
    full = lax.dot_general(
        tall,
        pick,
        (((1,), (1,)), ((), ())),
        precision=lax.Precision.HIGHEST,
        preferred_element_type=F32,
    )
    same = (
        lax.broadcasted_iota(jnp.int32, (cols, cols), 0) // nproj
        == lax.broadcasted_iota(jnp.int32, (cols, cols), 1) // nproj
    )
    couple[...] = jnp.where(same, full, 0.0)

    arrived(got_prev, s_part.at[0], r_part.at[0])
    arrived(got_own, s_part.at[1], r_part.at[1])
    for part, mine, other in ((0, part_own, got_own), (1, part_prev, got_prev)):
        weighted_out[part] = lax.dot_general(
            couple[...],
            mine[...] + other[...],
            (((1,), (1,)), ((), ())),
            precision=lax.Precision.HIGHEST,
            preferred_element_type=F32,
        )

    for side in range(2):
        arrived(halo.at[side], s_halo.at[side], r_halo.at[side])
    for copy in sent:
        copy.wait_send()
    for copy in stores:
        copy.wait()


def apply_terms(
    n_space,
    box_ref,
    weighted_ref,
    pre_ref,
    ion_ref,
    local_hbm,
    turned_hbm,
    halo_hbm,
    app_hbm,
    pot_ref,
    local_part,
    turned,
    halo,
    app_ref,
    scat,
    weights,
    added,
    nonlocal_part,
    s_turned,
    s_local,
    s_halo,
    s_app,
):
    orbs, planes, rows, cols = app_ref.shape
    cells = planes * rows
    wide = orbs * planes
    atoms2, square, depth = turned.shape
    atoms = atoms2 // 2
    width = planes
    nproj = depth // width
    me_s = lax.axis_index("space")
    prv = lax.rem(me_s + n_space - 1, n_space)
    firsts = (me_s * atoms, prv * atoms)
    pieces = s_turned.shape[0]
    lot = atoms2 // pieces
    batches = s_local.shape[0]
    some = orbs // batches

    loads_t = []
    for n in range(pieces):
        at = pl.ds(n * lot, lot)
        loads_t.append(pltpu.make_async_copy(turned_hbm.at[at], turned.at[at], s_turned.at[n]))
    loads_l = []
    for n in range(batches):
        at = pl.ds(n * some, some)
        loads_l.append(pltpu.make_async_copy(local_hbm.at[at], local_part.at[at], s_local.at[n]))
    load_h = pltpu.make_async_copy(halo_hbm, halo, s_halo)
    for copy in loads_t:
        copy.start()
    load_h.start()
    for copy in loads_l:
        copy.start()

    tables(box_ref, firsts[0], firsts[1], scat, atoms, cols)
    belongs = ownership(orbs, wide, planes)
    step = plane_steps(width, wide, planes)
    for part in range(2):
        weights[part] = jnp.dot(
            weighted_ref[part].astype(BF16), belongs, preferred_element_type=F32
        )
    pot_ref[...] = ion_ref[...] + pre_ref[...]
    for n in range(atoms2):
        if n % lot == 0:
            loads_t[n // lot].wait()
        part, a = n // atoms, n % atoms
        keep = step == lax.rem(box_ref[0, firsts[part] + a], planes) - part * planes
        rows_a = weights[part, a * nproj : (a + 1) * nproj, :].reshape(nproj, 1, wide)
        placed = jnp.where(keep[None], rows_a, 0.0)
        placed = placed.reshape(nproj * width, wide).astype(BF16)
        term = jnp.dot(turned[n], placed, preferred_element_type=F32).astype(BF16)
        for y in range(rows):
            added[y, n * SLOT : (n + 1) * SLOT, :] = term[y * SLOT : (y + 1) * SLOT, :]

    for y in range(rows):
        nonlocal_part[pl.ds(y, wide, stride=rows), :] = lax.dot_general(
            added[y], scat[...], (((0,), (0,)), ((), ())), preferred_element_type=F32
        )

    load_h.wait()
    outs = []
    scale = -0.5 / 12.0
    for n in range(batches):
        loads_l[n].wait()

        def finish(o, carry):
            near_low, far_low = halo[0, o, 1].astype(F32), halo[0, o, 0].astype(F32)
            near_up, far_up = halo[1, o, 0].astype(F32), halo[1, o, 1].astype(F32)
            edge = {
                0: scale * (16.0 * near_low - far_low),
                1: (-scale) * near_low,
                planes - 2: (-scale) * near_up,
                planes - 1: scale * (16.0 * near_up - far_up),
            }
            for i in range(planes):
                at = pl.ds(pl.multiple_of(o * cells + i * rows, rows), rows)
                total = local_part[o, i * rows : (i + 1) * rows, :] + nonlocal_part[at, :]
                if i in edge:
                    total = total + edge[i]
                app_ref[o, i] = total.astype(BF16)
            return carry

        lax.fori_loop(n * some, (n + 1) * some, finish, 0)
        at = pl.ds(n * some, some)
        outs.append(pltpu.make_async_copy(app_ref.at[at], app_hbm.at[at], s_app.at[n]))
        outs[n].start()
    for copy in outs:
        copy.wait()


def local(
    n_band,
    n_space,
    orbitals,
    occupations,
    potential_in,
    ionic_potential,
    hartree_prev,
    projectors,
    box_start,
    coupling,
):
    orbs, planes, rows, cols = orbitals.shape
    atoms, nproj, width, square = projectors.shape
    cells = planes * rows
    wide = orbs * planes
    group = 8 if n_space % 8 == 0 else 2
    n_far = n_space // group
    half = atoms // 2
    left, right = stencil_matrices(planes, rows, cols)
    left, right = jnp.asarray(left, BF16), jnp.asarray(right, BF16)
    vmem = pl.BlockSpec(memory_space=pltpu.VMEM)
    smem = pl.BlockSpec(memory_space=pltpu.SMEM)
    anywhere = pl.BlockSpec(memory_space=pl.ANY)
    dma = pltpu.SemaphoreType.DMA
    grid_f32 = jax.ShapeDtypeStruct(potential_in.shape, F32)
    halo_shape = (2, orbs, 2, rows, cols)
    turned_shape = (2 * atoms, square, nproj * width)
    scratch = [
        pltpu.VMEM(orbitals.shape, BF16),
        pltpu.VMEM(potential_in.shape, F32),
        pltpu.VMEM(hartree_prev.shape, F32),
        pltpu.VMEM(projectors.shape, BF16),
        pltpu.VMEM(left.shape, BF16),
        pltpu.VMEM(right.shape, BF16),
        pltpu.VMEM(projectors.shape, BF16),
        pltpu.VMEM((2, 2, rows, cols), F32),
        pltpu.VMEM((2, rows, cols), F32),
        pltpu.VMEM((planes, rows, cols), F32),
        pltpu.VMEM((planes, rows, cols), BF16),
        pltpu.VMEM((n_band, planes, rows, cols), BF16),
        pltpu.VMEM((planes, rows, cols), F32),
        pltpu.VMEM((ROWGROUP, cols), F32),
        pltpu.VMEM((ROWGROUP, cols), F32),
        pltpu.VMEM((ROWGROUP, cols), F32),
        pltpu.VMEM((n_band, ROWGROUP, cols), F32),
        pltpu.VMEM((group, ROWGROUP, cols), F32),
        pltpu.VMEM((n_far, ROWGROUP, cols), F32),
        pltpu.VMEM((2 * atoms * SLOT, cols), BF16),
        pltpu.VMEM((orbs, cells, cols), F32),
        pltpu.VMEM((orbs * cells, cols), F32),
        pltpu.VMEM((2 * atoms, square, wide), BF16),
        pltpu.VMEM(turned_shape, BF16),
        pltpu.VMEM((wide // cols, atoms * nproj * ROWGROUP, cols), F32),
        pltpu.VMEM((orbs, cols), F32),
        pltpu.VMEM((orbs, cols), F32),
        pltpu.VMEM((orbs, cols), F32),
        pltpu.VMEM((orbs, cols), F32),
        pltpu.VMEM((cols, cols), F32),
        pltpu.VMEM((planes + 2, rows, cols), F32),
        dma((6,)),
        dma((3,)),
        dma((half,)),
        dma((half,)),
        dma((half,)),
        dma((half,)),
        dma((2,)),
        dma((2,)),
        dma((2,)),
        dma((2,)),
        dma((n_band,)),
        dma((n_band,)),
        dma((n_band,)),
        dma((n_band,)),
        dma((group,)),
        dma((group,)),
        dma((n_far,)),
        dma((n_far,)),
        dma((2,)),
        dma((2,)),
        dma((2,)),
        dma((2,)),
    ]
    local_part, turned, halo, weighted, pre = pl.pallas_call(
        functools.partial(exchange, (n_band, n_space, group)),
        out_shape=(
            jax.ShapeDtypeStruct((orbs, cells, cols), F32),
            jax.ShapeDtypeStruct(turned_shape, BF16),
            jax.ShapeDtypeStruct(halo_shape, BF16),
            jax.ShapeDtypeStruct((2, cols, orbs), F32),
            grid_f32,
        ),
        in_specs=[smem, smem, vmem] + [anywhere] * 6,
        out_specs=(anywhere, anywhere, anywhere, vmem, vmem),
        scratch_shapes=scratch,
        compiler_params=pltpu.CompilerParams(
            collective_id=0, has_side_effects=True, vmem_limit_bytes=60 * 1024 * 1024
        ),
    )(
        box_start,
        occupations,
        coupling,
        orbitals,
        potential_in,
        hartree_prev,
        projectors,
        left,
        right,
    )
    return pl.pallas_call(
        functools.partial(apply_terms, n_space),
        out_shape=(jax.ShapeDtypeStruct(orbitals.shape, BF16), grid_f32),
        in_specs=[smem, vmem, vmem, vmem, anywhere, anywhere, anywhere],
        out_specs=(anywhere, vmem),
        scratch_shapes=[
            pltpu.VMEM((orbs, cells, cols), F32),
            pltpu.VMEM(turned_shape, BF16),
            pltpu.VMEM(halo_shape, BF16),
            pltpu.VMEM(orbitals.shape, BF16),
            pltpu.VMEM((2 * atoms * SLOT, cols), BF16),
            pltpu.VMEM((2, cols, wide), F32),
            pltpu.VMEM((rows, 2 * atoms * SLOT, wide), BF16),
            pltpu.VMEM((orbs * cells, cols), F32),
            dma((4,)),
            dma((4,)),
            dma,
            dma((4,)),
        ],
        compiler_params=pltpu.CompilerParams(vmem_limit_bytes=60 * 1024 * 1024),
    )(box_start, weighted, pre, ionic_potential, local_part, turned, halo)


def solution(mesh):
    return jax.shard_map(
        functools.partial(local, mesh.shape["band"], mesh.shape["space"]),
        mesh=mesh,
        in_specs=(
            P("band", "space", None, None),
            P("band"),
            P("space", None, None),
            P("space", None, None),
            P("space", None, None),
            P("space", None, None, None),
            P(),
            P(),
        ),
        out_specs=(P("band", "space", None, None), P("space", None, None)),
        check_vma=False,
    )
```

time: 50.8 us -> 45.4 us (0.89)
  local copies, waits for them, and re-layouts: 3.65 us -> 0 us
  Pallas kernels: 46.4 us -> 44.6 us
    unnamed x4 -> x0, local copies, waits for them, and re-layouts: 3.65 us -> none
    pallas_call x1 -> x2, Pallas kernels: 46.4 us -> 44.6 us  [the longest x1 37.3 us: local(): pl.pallas_call(functools.partial(exchange, (n_band, n_space, group)), out...]
where the time goes in v3:
time: 45.4 us; the launch traced here: 45.3 us
  Pallas kernels  44.6 us (98%)
  between operations  0.64 us (1%)
    pallas_call x1, Pallas kernels, local(): pl.pallas_call(functools.partial(exchange, (n_band, n_space, group)), out...  37.3 us
    pallas_call x1, Pallas kernels, local(): pl.pallas_call(functools.partial(apply_terms, n_space), out_shape=(jax.Sh...  7.33 us

profile of v3, /device:TPU:1, one launch (start us, length us, event | category | flops | bytes accessed | tf_op | source)
XLA Modules:
  0.0 45.3 jit_solution(18021627006323157116)
XLA Ops:
  0.6 37.3 %shard_map.113 = (f32[24,256,128]{2,1,0:T(8,128)}, bf16[16,256,208]{2,1,0:T(8,128)(2,1)}, bf16[2,24,2,16,128]{4,3,2,1,0:T(8,128)(2,1)}, f32[2,128,24]{2,1,0:T(8,128)}, f32[16,16,128]{2,1,0:T(8,128)}) custom-call(s32[3,512]{1,0:T(4,128)} %box_ref.3, f32[24]{0:T(128)} %occ_ref.1, f32[13,13]{1,0:T(8,128)} %coup_ref.1, bf16[24,16,16,128]{3,2,1,0:T(8,128)(2,1)} %orb_hbm.1, ...), custom_call_target="tpu_custom_call" | custom-call | tf_op jit(solution)/shard_map/pallas_call | solution.py:633
  37.9 7.3 %shard_map.114 = (bf16[24,16,16,128]{3,2,1,0:T(8,128)(2,1)}, f32[16,16,128]{2,1,0:T(8,128)}) custom-call(s32[3,512]{1,0:T(4,128)} %box_ref.3, f32[2,128,24]{2,1,0:T(8,128)} %get-tuple-element.7.weighted_ref, f32[16,16,128]{2,1,0:T(8,128)} %get-tuple-element.8.pre_ref, f32[16,16,128]{2,1,0:T(8,128)} %ion_ref.1, f32[24,256,128]{2,1,0:T(8,128)} %get-tuple-element.9.local_hbm, ...), custom_call_target="tpu_custom_call" | custom-call | tf_op jit(solution)/shard_map/pallas_call | solution.py:659

commit v4 on v3

--- a/solution.py
+++ b/solution.py
@@ -68,8 +68,8 @@
     proj_hbm,
     left_hbm,
     right_hbm,
-    local_out,
-    turned_out,
+    local_part,
+    turned,
     halo,
     weighted_out,
     pre_ref,
@@ -93,10 +93,8 @@
     chg_in2,
     chg_in3,
     scat,
-    local_part,
     fields,
     gathered,
-    turned,
     partial,
     part_own,
     part_prev,
@@ -105,11 +103,14 @@
     couple,
     hone,
     s_load,
-    s_store,
     s_proj,
     r_proj,
     s_fwd,
     r_fwd,
+    s_across,
+    r_across,
+    s_last,
+    r_last,
     s_halo,
     r_halo,
     s_hh,
@@ -133,7 +134,7 @@
     cells = planes * rows
     wide = orbs * planes
     n_far = n_space // group
-    half = atoms // 2
+    share = atoms // n_band
 
     me_b = lax.axis_index("band")
     me_s = lax.axis_index("space")
@@ -141,17 +142,19 @@
     prv = lax.rem(me_s + n_space - 1, n_space)
     core = lax.rem(me_b, 2)
     sib = me_b + 1 - 2 * core
-    near = lax.rem(me_s, group)
-    far = me_s // group
+    across = lax.rem(me_b + 2, n_band)
+    beyond = lax.rem(sib + 2, n_band)
+    near = me_s // n_far
+    far = lax.rem(me_s, n_far)
 
     def band_peer(d):
         return (lax.rem(me_b + d, n_band), me_s)
 
     def near_peer(d):
-        return (me_b, far * group + lax.rem(near + d, group))
+        return (me_b, lax.rem(near + d, group) * n_far + far)
 
     def far_peer(d):
-        return (me_b, lax.rem(far + d, n_far) * group + near)
+        return (me_b, near * n_far + lax.rem(far + d, n_far))
 
     partners = [(me_b, nxt), (me_b, prv)]
     partners += [band_peer(d) for d in range(1, n_band)]
@@ -201,9 +204,11 @@
             device_id_type=MESH,
         ).wait_recv()
 
-    for h in range(half):
-        a = core * half + h
+    def send_projectors(h):
+        a = me_b * share + h
         send(proj_hbm.at[a], pprev.at[a], s_proj.at[h], r_proj.at[h], (me_b, nxt))
+
+    send_projectors(0)
     send(har_hbm.at[pl.ds(0, 2)], hhalo.at[1], s_hh.at[1], r_hh.at[1], (me_b, prv))
     send(har_hbm.at[pl.ds(planes - 2, 2)], hhalo.at[0], s_hh.at[0], r_hh.at[0], (me_b, nxt))
     first_own = me_s * atoms
@@ -226,12 +231,14 @@
         return charge
 
     chg1[...] = lax.fori_loop(0, planes, density_plane, jnp.zeros((ROWGROUP, cols), F32))
-    for d in range(1, n_band):
-        send(chg1, chg_in1.at[me_b], s_c1.at[d], r_c1.at[me_b], band_peer(d))
+    for d in range(1, group):
+        send(chg1, chg_in2.at[near], s_c2.at[d], r_c2.at[near], near_peer(d))
+    for h in range(1, share):
+        send_projectors(h)
     for d in range(1, n_band):
         send(dens_b, dens_in.at[me_b], s_dens.at[d], r_dens.at[me_b], band_peer(d))
+
     send(orb_ref.at[:, pl.ds(0, 2)], halo.at[1], s_halo.at[1], r_halo.at[1], (me_b, prv))
-    send(orb_ref.at[:, pl.ds(planes - 2, 2)], halo.at[0], s_halo.at[0], r_halo.at[0], (me_b, nxt))
 
     for y in range(rows):
         line = fields[pl.ds(y, wide, stride=rows), :].astype(BF16)
@@ -240,16 +247,6 @@
         ).astype(BF16)
         for n in range(2 * atoms):
             gathered[n, y * SLOT : (y + 1) * SLOT, :] = cut[n * SLOT : (n + 1) * SLOT, :]
-
-    for d in range(1, n_band):
-        peer = lax.rem(me_b + d, n_band)
-        arrived(chg_in1.at[peer], s_c1.at[d], r_c1.at[peer])
-    charge = chg1[...]
-    for d in range(1, n_band):
-        charge = charge + chg_in1[lax.rem(me_b + d, n_band)]
-    chg2[...] = charge
-    for d in range(1, group):
-        send(chg2, chg_in2.at[near], s_c2.at[d], r_c2.at[near], near_peer(d))
 
     belongs = ownership(orbs, wide, planes)
     step = plane_steps(width, wide, planes)
@@ -284,21 +281,41 @@
         ) + lax.dot_general(belongs, low, lanes, preferred_element_type=F32)
 
     def hand_on(h):
-        a = core * half + h
+        a = me_b * share + h
         arrived(pprev.at[a], s_proj.at[h], r_proj.at[h])
+        send(pprev.at[a], pprev.at[a], s_across.at[h], r_across.at[h], (across, me_s))
         send(pprev.at[a], pprev.at[a], s_fwd.at[h], r_fwd.at[h], (sib, me_s))
 
+    def hand_across(h):
+        a = across * share + h
+        arrived(pprev.at[a], s_across.at[h], r_across.at[h])
+        send(pprev.at[a], pprev.at[a], s_last.at[h], r_last.at[h], (sib, me_s))
+
+    hand_on(0)
     loads[1].wait()
     for a in range(atoms):
         gather(0, proj_ref, first_own, a)
     part_own[...] = gathered_sum()
     send(part_own, got_prev, s_part.at[0], r_part.at[0], (me_b, nxt))
 
-    hand_on(0)
+    hand_on(1)
+
+    for d in range(1, group):
+        peer = lax.rem(near + d, group)
+        arrived(chg_in2.at[peer], s_c2.at[d], r_c2.at[peer])
+    charge = chg1[...]
+    for d in range(1, group):
+        charge = charge + chg_in2[lax.rem(near + d, group)]
+    chg2[...] = charge
+    for d in range(1, n_far):
+        send(chg2, chg_in3.at[far], s_c3.at[d], r_c3.at[far], far_peer(d))
+    send(orb_ref.at[:, pl.ds(planes - 2, 2)], halo.at[0], s_halo.at[0], r_halo.at[0], (me_b, nxt))
 
     for n in range(2, 5):
         loads[n].wait()
     for pair in range(orbs // 2):
+        if pair == orbs // 4:
+            hand_across(0)
         first, second = orb_ref[2 * pair], orb_ref[2 * pair + 1]
         both = jnp.concatenate([first.reshape(cells, cols), second.reshape(cells, cols)], axis=1)
         lap = jnp.dot(left_ref[...], both, preferred_element_type=F32)
@@ -307,19 +324,7 @@
         for n in range(2):
             field = both[:, n * cols : (n + 1) * cols].astype(F32)
             local_part[2 * pair + n] = lap[:, n * cols : (n + 1) * cols] * (-0.5 / 12.0) + vin * field
-    stores = [
-        pltpu.make_async_copy(local_part, local_out, s_store.at[0]),
-        pltpu.make_async_copy(
-            turned.at[pl.ds(0, atoms)], turned_out.at[pl.ds(0, atoms)], s_store.at[1]
-        ),
-        pltpu.make_async_copy(
-            turned.at[pl.ds(atoms, atoms)], turned_out.at[pl.ds(atoms, atoms)], s_store.at[2]
-        ),
-    ]
-    stores[0].start()
-    stores[1].start()
-
-    hand_on(1)
+    hand_across(1)
 
     for d in range(1, n_band):
         peer = lax.rem(me_b + d, n_band)
@@ -330,28 +335,26 @@
     rho[...] = total_density
     send(rho.at[0], rhalo.at[1], s_rh.at[1], r_rh.at[1], (me_b, prv))
     send(rho.at[planes - 1], rhalo.at[0], s_rh.at[0], r_rh.at[0], (me_b, nxt))
-    for d in range(1, group):
-        peer = lax.rem(near + d, group)
-        arrived(chg_in2.at[peer], s_c2.at[d], r_c2.at[peer])
+    for d in range(1, n_far):
+        peer = lax.rem(far + d, n_far)
+        arrived(chg_in3.at[peer], s_c3.at[d], r_c3.at[peer])
     charge = chg2[...]
-    for d in range(1, group):
-        charge = charge + chg_in2[lax.rem(near + d, group)]
+    for d in range(1, n_far):
+        charge = charge + chg_in3[lax.rem(far + d, n_far)]
     chg3[...] = charge
-    for d in range(1, n_far):
-        send(chg3, chg_in3.at[far], s_c3.at[d], r_c3.at[far], far_peer(d))
-
-    for h in range(2, half):
-        hand_on(h)
-        gather(1, pprev, first_prev, core * half + h - 2)
-    for h in range(half):
-        a = (1 - core) * half + h
-        arrived(pprev.at[a], s_fwd.at[h], r_fwd.at[h])
-        gather(1, pprev, first_prev, a)
-        if h < 2:
-            gather(1, pprev, first_prev, core * half + half - 2 + h)
+    for d in range(1, n_band):
+        send(chg3, chg_in1.at[me_b], s_c1.at[d], r_c1.at[me_b], band_peer(d))
+
+    for base in (me_b, across):
+        for h in range(share):
+            gather(1, pprev, first_prev, base * share + h)
+    for base, send_sem, recv_sem in ((sib, s_fwd, r_fwd), (beyond, s_last, r_last)):
+        for h in range(share):
+            a = base * share + h
+            arrived(pprev.at[a], send_sem.at[h], recv_sem.at[h])
+            gather(1, pprev, first_prev, a)
     part_prev[...] = gathered_sum()
     send(part_prev, got_own, s_part.at[1], r_part.at[1], (me_b, prv))
-    stores[2].start()
 
     loads[5].wait()
     for side in range(2):
@@ -384,12 +387,12 @@
     for p in range(-1, planes + 1):
         total = start_plane(p - 1) + start_plane(p + 1) + around(start_plane(p))
         hone[p + 1] = (total + FOUR_PI * rho_plane(p)) * inverse
-    for d in range(1, n_far):
-        peer = lax.rem(far + d, n_far)
-        arrived(chg_in3.at[peer], s_c3.at[d], r_c3.at[peer])
+    for d in range(1, n_band):
+        peer = lax.rem(me_b + d, n_band)
+        arrived(chg_in1.at[peer], s_c1.at[d], r_c1.at[peer])
     charge = chg3[...]
-    for d in range(1, n_far):
-        charge = charge + chg_in3[lax.rem(far + d, n_far)]
+    for d in range(1, n_band):
+        charge = charge + chg_in1[lax.rem(me_b + d, n_band)]
     mean = jnp.sum(charge, axis=(0, 1), keepdims=True) * (1.0 / (cells * cols * n_space))
     lift = FOUR_PI * inverse * (1.0 + 6.0 * inverse) * mean
     for p in range(planes):
@@ -433,8 +436,6 @@
         arrived(halo.at[side], s_halo.at[side], r_halo.at[side])
     for copy in sent:
         copy.wait_send()
-    for copy in stores:
-        copy.wait()
 
 
 def apply_terms(
@@ -443,22 +444,16 @@
     weighted_ref,
     pre_ref,
     ion_ref,
-    local_hbm,
-    turned_hbm,
-    halo_hbm,
-    app_hbm,
-    pot_ref,
     local_part,
     turned,
     halo,
+    app_hbm,
+    pot_ref,
     app_ref,
     scat,
     weights,
     added,
     nonlocal_part,
-    s_turned,
-    s_local,
-    s_halo,
     s_app,
 ):
     orbs, planes, rows, cols = app_ref.shape
@@ -471,25 +466,9 @@
     me_s = lax.axis_index("space")
     prv = lax.rem(me_s + n_space - 1, n_space)
     firsts = (me_s * atoms, prv * atoms)
-    pieces = s_turned.shape[0]
-    lot = atoms2 // pieces
-    batches = s_local.shape[0]
+    batches = s_app.shape[0]
     some = orbs // batches
 
-    loads_t = []
-    for n in range(pieces):
-        at = pl.ds(n * lot, lot)
-        loads_t.append(pltpu.make_async_copy(turned_hbm.at[at], turned.at[at], s_turned.at[n]))
-    loads_l = []
-    for n in range(batches):
-        at = pl.ds(n * some, some)
-        loads_l.append(pltpu.make_async_copy(local_hbm.at[at], local_part.at[at], s_local.at[n]))
-    load_h = pltpu.make_async_copy(halo_hbm, halo, s_halo)
-    for copy in loads_t:
-        copy.start()
-    load_h.start()
-    for copy in loads_l:
-        copy.start()
 
     tables(box_ref, firsts[0], firsts[1], scat, atoms, cols)
     belongs = ownership(orbs, wide, planes)
@@ -500,8 +479,6 @@
         )
     pot_ref[...] = ion_ref[...] + pre_ref[...]
     for n in range(atoms2):
-        if n % lot == 0:
-            loads_t[n // lot].wait()
         part, a = n // atoms, n % atoms
         keep = step == lax.rem(box_ref[0, firsts[part] + a], planes) - part * planes
         rows_a = weights[part, a * nproj : (a + 1) * nproj, :].reshape(nproj, 1, wide)
@@ -516,11 +493,9 @@
             added[y], scat[...], (((0,), (0,)), ((), ())), preferred_element_type=F32
         )
 
-    load_h.wait()
     outs = []
     scale = -0.5 / 12.0
     for n in range(batches):
-        loads_l[n].wait()
 
         def finish(o, carry):
             near_low, far_low = halo[0, o, 1].astype(F32), halo[0, o, 0].astype(F32)
@@ -565,7 +540,7 @@
     wide = orbs * planes
     group = 8 if n_space % 8 == 0 else 2
     n_far = n_space // group
-    half = atoms // 2
+    share = atoms // n_band
     left, right = stencil_matrices(planes, rows, cols)
     left, right = jnp.asarray(left, BF16), jnp.asarray(right, BF16)
     vmem = pl.BlockSpec(memory_space=pltpu.VMEM)
@@ -596,10 +571,8 @@
         pltpu.VMEM((group, ROWGROUP, cols), F32),
         pltpu.VMEM((n_far, ROWGROUP, cols), F32),
         pltpu.VMEM((2 * atoms * SLOT, cols), BF16),
-        pltpu.VMEM((orbs, cells, cols), F32),
         pltpu.VMEM((orbs * cells, cols), F32),
         pltpu.VMEM((2 * atoms, square, wide), BF16),
-        pltpu.VMEM(turned_shape, BF16),
         pltpu.VMEM((wide // cols, atoms * nproj * ROWGROUP, cols), F32),
         pltpu.VMEM((orbs, cols), F32),
         pltpu.VMEM((orbs, cols), F32),
@@ -608,11 +581,14 @@
         pltpu.VMEM((cols, cols), F32),
         pltpu.VMEM((planes + 2, rows, cols), F32),
         dma((6,)),
-        dma((3,)),
-        dma((half,)),
-        dma((half,)),
-        dma((half,)),
-        dma((half,)),
+        dma((share,)),
+        dma((share,)),
+        dma((share,)),
+        dma((share,)),
+        dma((share,)),
+        dma((share,)),
+        dma((share,)),
+        dma((share,)),
         dma((2,)),
         dma((2,)),
         dma((2,)),
@@ -630,20 +606,20 @@
         dma((2,)),
         dma((2,)),
     ]
-    local_part, turned, halo, weighted, pre = pl.pallas_call(
+    handed = pl.pallas_call(
         functools.partial(exchange, (n_band, n_space, group)),
         out_shape=(
-            jax.ShapeDtypeStruct((orbs, cells, cols), F32),
-            jax.ShapeDtypeStruct(turned_shape, BF16),
-            jax.ShapeDtypeStruct(halo_shape, BF16),
-            jax.ShapeDtypeStruct((2, cols, orbs), F32),
-            grid_f32,
+            pltpu.VMEM((orbs, cells, cols), F32),
+            pltpu.VMEM(turned_shape, BF16),
+            pltpu.VMEM(halo_shape, BF16),
+            pltpu.VMEM((2, cols, orbs), F32),
+            pltpu.VMEM(potential_in.shape, F32),
         ),
         in_specs=[smem, smem, vmem] + [anywhere] * 6,
-        out_specs=(anywhere, anywhere, anywhere, vmem, vmem),
+        out_specs=(vmem,) * 5,
         scratch_shapes=scratch,
         compiler_params=pltpu.CompilerParams(
-            collective_id=0, has_side_effects=True, vmem_limit_bytes=60 * 1024 * 1024
+            collective_id=0, has_side_effects=True, vmem_limit_bytes=54 * 1024 * 1024
         ),
     )(
         box_start,
@@ -656,26 +632,23 @@
         left,
         right,
     )
+    local_part, turned, halo, weighted, pre = (
+        pltpu.with_memory_space_constraint(array, pltpu.VMEM) for array in handed
+    )
     return pl.pallas_call(
         functools.partial(apply_terms, n_space),
         out_shape=(jax.ShapeDtypeStruct(orbitals.shape, BF16), grid_f32),
-        in_specs=[smem, vmem, vmem, vmem, anywhere, anywhere, anywhere],
+        in_specs=[smem] + [vmem] * 6,
         out_specs=(anywhere, vmem),
         scratch_shapes=[
-            pltpu.VMEM((orbs, cells, cols), F32),
-            pltpu.VMEM(turned_shape, BF16),
-            pltpu.VMEM(halo_shape, BF16),
             pltpu.VMEM(orbitals.shape, BF16),
             pltpu.VMEM((2 * atoms * SLOT, cols), BF16),
             pltpu.VMEM((2, cols, wide), F32),
             pltpu.VMEM((rows, 2 * atoms * SLOT, wide), BF16),
             pltpu.VMEM((orbs * cells, cols), F32),
             dma((4,)),
-            dma((4,)),
-            dma,
-            dma((4,)),
         ],
-        compiler_params=pltpu.CompilerParams(vmem_limit_bytes=60 * 1024 * 1024),
+        compiler_params=pltpu.CompilerParams(vmem_limit_bytes=54 * 1024 * 1024),
     )(box_start, weighted, pre, ionic_potential, local_part, turned, halo)
 
 

time: 45.4 us -> 38.8 us (0.85)
  the two profiles are of different devices: /device:TPU:1 before, /device:TPU:24 now
where the time goes in v4:
time: 38.8 us; the launch traced here: 38.3 us
  Pallas kernels  37.7 us (97%)
  between operations  0.64 us (2%)
    pallas_call x1, Pallas kernels, local(): pl.pallas_call(functools.partial(exchange, (n_band, n_space, group)), out...  32 us
    pallas_call x1, Pallas kernels, local(): pl.pallas_call(functools.partial(apply_terms, n_space), out_shape=(jax.Sh...  5.64 us

profile of v4, /device:TPU:24, one launch (start us, length us, event | category | flops | bytes accessed | tf_op | source)
XLA Modules:
  0.0 38.3 jit_solution(16288083564655198578)
XLA Ops:
  0.6 32.0 %shard_map.113 = (f32[24,256,128]{2,1,0:T(8,128)S(1)}, bf16[16,256,208]{2,1,0:T(8,128)(2,1)S(1)}, bf16[2,24,2,16,128]{4,3,2,1,0:T(8,128)(2,1)S(1)}, f32[2,128,24]{2,1,0:T(8,128)S(1)}, f32[16,16,128]{2,1,0:T(8,128)S(1)}) custom-call(s32[3,512]{1,0:T(4,128)} %box_ref.3, f32[24]{0:T(128)} %occ_ref.1, f32[13,13]{1,0:T(8,128)} %coup_ref.1, ...), custom_call_target="tpu_custom_call" | custom-call | tf_op jit(solution)/shard_map/pallas_call | solution.py:609
  32.7 5.6 %shard_map.114 = (bf16[24,16,16,128]{3,2,1,0:T(8,128)(2,1)}, f32[16,16,128]{2,1,0:T(8,128)}) custom-call(s32[3,512]{1,0:T(4,128)} %box_ref.3, f32[2,128,24]{2,1,0:T(8,128)S(1)} %get-tuple-element.7.weighted_ref, f32[16,16,128]{2,1,0:T(8,128)S(1)} %get-tuple-element.8.pre_ref, f32[16,16,128]{2,1,0:T(8,128)} %ion_ref.1, ...), custom_call_target="tpu_custom_call" | custom-call | tf_op jit(solution)/shard_map/pallas_call | solution.py:638

commit v5 on v4

--- a/solution.py
+++ b/solution.py
@@ -69,9 +69,9 @@
     left_hbm,
     right_hbm,
     local_part,
-    turned,
+    fields,
     halo,
-    weighted_out,
+    charge_out,
     pre_ref,
     orb_ref,
     vin_ref,
@@ -93,9 +93,11 @@
     chg_in2,
     chg_in3,
     scat,
-    fields,
     gathered,
+    turned,
     partial,
+    weights,
+    added,
     part_own,
     part_prev,
     got_own,
@@ -387,19 +389,11 @@
     for p in range(-1, planes + 1):
         total = start_plane(p - 1) + start_plane(p + 1) + around(start_plane(p))
         hone[p + 1] = (total + FOUR_PI * rho_plane(p)) * inverse
-    for d in range(1, n_band):
-        peer = lax.rem(me_b + d, n_band)
-        arrived(chg_in1.at[peer], s_c1.at[d], r_c1.at[peer])
-    charge = chg3[...]
-    for d in range(1, n_band):
-        charge = charge + chg_in1[lax.rem(me_b + d, n_band)]
-    mean = jnp.sum(charge, axis=(0, 1), keepdims=True) * (1.0 / (cells * cols * n_space))
-    lift = FOUR_PI * inverse * (1.0 + 6.0 * inverse) * mean
     for p in range(planes):
         total = hone[p] + hone[p + 2] + around(hone[p + 1])
         second = (total + FOUR_PI * rho[p]) * inverse
         root = jnp.exp(jnp.log(rho[p] * (3.0 / math.pi)) * (1.0 / 3.0))
-        pre_ref[p] = (second - lift) - root
+        pre_ref[p] = second - root
 
     row_id = lax.broadcasted_iota(jnp.int32, (cols, nproj), 0) % nproj
     pick = jnp.where(
@@ -424,80 +418,64 @@
     arrived(got_prev, s_part.at[0], r_part.at[0])
     arrived(got_own, s_part.at[1], r_part.at[1])
     for part, mine, other in ((0, part_own, got_own), (1, part_prev, got_prev)):
-        weighted_out[part] = lax.dot_general(
+        weighted = lax.dot_general(
             couple[...],
             mine[...] + other[...],
             (((1,), (1,)), ((), ())),
             precision=lax.Precision.HIGHEST,
             preferred_element_type=F32,
-        )
-
-    for side in range(2):
-        arrived(halo.at[side], s_halo.at[side], r_halo.at[side])
-    for copy in sent:
-        copy.wait_send()
-
-
-def apply_terms(
-    n_space,
-    box_ref,
-    weighted_ref,
-    pre_ref,
-    ion_ref,
-    local_part,
-    turned,
-    halo,
-    app_hbm,
-    pot_ref,
-    app_ref,
-    scat,
-    weights,
-    added,
-    nonlocal_part,
-    s_app,
-):
-    orbs, planes, rows, cols = app_ref.shape
-    cells = planes * rows
-    wide = orbs * planes
-    atoms2, square, depth = turned.shape
-    atoms = atoms2 // 2
-    width = planes
-    nproj = depth // width
-    me_s = lax.axis_index("space")
-    prv = lax.rem(me_s + n_space - 1, n_space)
-    firsts = (me_s * atoms, prv * atoms)
-    batches = s_app.shape[0]
-    some = orbs // batches
-
-
-    tables(box_ref, firsts[0], firsts[1], scat, atoms, cols)
-    belongs = ownership(orbs, wide, planes)
-    step = plane_steps(width, wide, planes)
-    for part in range(2):
-        weights[part] = jnp.dot(
-            weighted_ref[part].astype(BF16), belongs, preferred_element_type=F32
-        )
-    pot_ref[...] = ion_ref[...] + pre_ref[...]
-    for n in range(atoms2):
+        ).astype(BF16)
+        weights[part] = jnp.dot(weighted, belongs, preferred_element_type=F32)
+
+    for n in range(2 * atoms):
         part, a = n // atoms, n % atoms
-        keep = step == lax.rem(box_ref[0, firsts[part] + a], planes) - part * planes
+        first = (first_own, first_prev)[part]
+        keep = step == lax.rem(box_ref[0, first + a], planes) - part * planes
         rows_a = weights[part, a * nproj : (a + 1) * nproj, :].reshape(nproj, 1, wide)
         placed = jnp.where(keep[None], rows_a, 0.0)
         placed = placed.reshape(nproj * width, wide).astype(BF16)
         term = jnp.dot(turned[n], placed, preferred_element_type=F32).astype(BF16)
         for y in range(rows):
             added[y, n * SLOT : (n + 1) * SLOT, :] = term[y * SLOT : (y + 1) * SLOT, :]
-
     for y in range(rows):
-        nonlocal_part[pl.ds(y, wide, stride=rows), :] = lax.dot_general(
+        fields[pl.ds(y, wide, stride=rows), :] = lax.dot_general(
             added[y], scat[...], (((0,), (0,)), ((), ())), preferred_element_type=F32
         )
 
+    for d in range(1, n_band):
+        peer = lax.rem(me_b + d, n_band)
+        arrived(chg_in1.at[peer], s_c1.at[d], r_c1.at[peer])
+    charge = chg3[...]
+    for d in range(1, n_band):
+        charge = charge + chg_in1[lax.rem(me_b + d, n_band)]
+    charge_out[...] = charge
+    for side in range(2):
+        arrived(halo.at[side], s_halo.at[side], r_halo.at[side])
+    for copy in sent:
+        copy.wait_send()
+
+
+def finish_terms(
+    n_space,
+    local_part,
+    nonlocal_part,
+    halo,
+    charge_ref,
+    pre_ref,
+    ion_ref,
+    app_hbm,
+    pot_ref,
+    app_ref,
+    s_app,
+):
+    orbs, planes, rows, cols = app_ref.shape
+    cells = planes * rows
+    batches = s_app.shape[0]
+    some = orbs // batches
+    scale = -0.5 / 12.0
     outs = []
-    scale = -0.5 / 12.0
     for n in range(batches):
-
-        def finish(o, carry):
+        for o in range(n * some, (n + 1) * some):
             near_low, far_low = halo[0, o, 1].astype(F32), halo[0, o, 0].astype(F32)
             near_up, far_up = halo[1, o, 0].astype(F32), halo[1, o, 1].astype(F32)
             edge = {
@@ -507,17 +485,21 @@
                 planes - 1: scale * (16.0 * near_up - far_up),
             }
             for i in range(planes):
-                at = pl.ds(pl.multiple_of(o * cells + i * rows, rows), rows)
-                total = local_part[o, i * rows : (i + 1) * rows, :] + nonlocal_part[at, :]
+                at = o * cells + i * rows
+                total = local_part[o, i * rows : (i + 1) * rows, :]
+                total = total + nonlocal_part[at : at + rows, :]
                 if i in edge:
                     total = total + edge[i]
                 app_ref[o, i] = total.astype(BF16)
-            return carry
-
-        lax.fori_loop(n * some, (n + 1) * some, finish, 0)
         at = pl.ds(n * some, some)
         outs.append(pltpu.make_async_copy(app_ref.at[at], app_hbm.at[at], s_app.at[n]))
         outs[n].start()
+
+    inverse = 1.0 / (6.0 + SCREENING)
+    mean = jnp.sum(charge_ref[...], axis=(0, 1), keepdims=True) * (1.0 / (cells * cols * n_space))
+    lift = FOUR_PI * inverse * (1.0 + 6.0 * inverse) * mean
+    for p in range(planes):
+        pot_ref[p] = ion_ref[p] + (pre_ref[p] - lift)
     for copy in outs:
         copy.wait()
 
@@ -571,9 +553,11 @@
         pltpu.VMEM((group, ROWGROUP, cols), F32),
         pltpu.VMEM((n_far, ROWGROUP, cols), F32),
         pltpu.VMEM((2 * atoms * SLOT, cols), BF16),
-        pltpu.VMEM((orbs * cells, cols), F32),
         pltpu.VMEM((2 * atoms, square, wide), BF16),
+        pltpu.VMEM(turned_shape, BF16),
         pltpu.VMEM((wide // cols, atoms * nproj * ROWGROUP, cols), F32),
+        pltpu.VMEM((2, cols, wide), F32),
+        pltpu.VMEM((rows, 2 * atoms * SLOT, wide), BF16),
         pltpu.VMEM((orbs, cols), F32),
         pltpu.VMEM((orbs, cols), F32),
         pltpu.VMEM((orbs, cols), F32),
@@ -610,9 +594,9 @@
         functools.partial(exchange, (n_band, n_space, group)),
         out_shape=(
             pltpu.VMEM((orbs, cells, cols), F32),
-            pltpu.VMEM(turned_shape, BF16),
+            pltpu.VMEM((orbs * cells, cols), F32),
             pltpu.VMEM(halo_shape, BF16),
-            pltpu.VMEM((2, cols, orbs), F32),
+            pltpu.VMEM((ROWGROUP, cols), F32),
             pltpu.VMEM(potential_in.shape, F32),
         ),
         in_specs=[smem, smem, vmem] + [anywhere] * 6,
@@ -632,24 +616,15 @@
         left,
         right,
     )
-    local_part, turned, halo, weighted, pre = (
-        pltpu.with_memory_space_constraint(array, pltpu.VMEM) for array in handed
-    )
+    handed = [pltpu.with_memory_space_constraint(array, pltpu.VMEM) for array in handed]
     return pl.pallas_call(
-        functools.partial(apply_terms, n_space),
+        functools.partial(finish_terms, n_space),
         out_shape=(jax.ShapeDtypeStruct(orbitals.shape, BF16), grid_f32),
-        in_specs=[smem] + [vmem] * 6,
+        in_specs=[vmem] * 6,
         out_specs=(anywhere, vmem),
-        scratch_shapes=[
-            pltpu.VMEM(orbitals.shape, BF16),
-            pltpu.VMEM((2 * atoms * SLOT, cols), BF16),
-            pltpu.VMEM((2, cols, wide), F32),
-            pltpu.VMEM((rows, 2 * atoms * SLOT, wide), BF16),
-            pltpu.VMEM((orbs * cells, cols), F32),
-            dma((4,)),
-        ],
+        scratch_shapes=[pltpu.VMEM(orbitals.shape, BF16), dma((4,))],
         compiler_params=pltpu.CompilerParams(vmem_limit_bytes=54 * 1024 * 1024),
-    )(box_start, weighted, pre, ionic_potential, local_part, turned, halo)
+    )(*handed, ionic_potential)
 
 
 def solution(mesh):

time: 38.8 us -> 38.3 us (0.987)
  Pallas kernels: 37.7 us -> 37.1 us
    pallas_call x1, Pallas kernels: 5.64 us -> 2.83 us  [local(): pl.pallas_call(functools.partial(finish_terms, n_space), out_shape=(jax.S...]
    pallas_call x1, Pallas kernels: 32 us -> 34.3 us  [local(): pl.pallas_call(functools.partial(exchange, (n_band, n_space, group)), out...]
where the time goes in v5:
time: 38.3 us; the launch traced here: 37.8 us
  Pallas kernels  37.1 us (97%)
  between operations  0.64 us (2%)
    pallas_call x1, Pallas kernels, local(): pl.pallas_call(functools.partial(exchange, (n_band, n_space, group)), out...  34.3 us
    pallas_call x1, Pallas kernels, local(): pl.pallas_call(functools.partial(finish_terms, n_space), out_shape=(jax.S...  2.83 us

profile of v5, /device:TPU:24, one launch (start us, length us, event | category | flops | bytes accessed | tf_op | source)
XLA Modules:
  0.0 37.8 jit_solution(10659470013498159037)
XLA Ops:
  0.6 34.3 %shard_map.113 = (f32[24,256,128]{2,1,0:T(8,128)S(1)}, f32[6144,128]{1,0:T(8,128)S(1)}, bf16[2,24,2,16,128]{4,3,2,1,0:T(8,128)(2,1)S(1)}, f32[8,128]{1,0:T(8,128)S(1)}, f32[16,16,128]{2,1,0:T(8,128)S(1)}) custom-call(s32[3,512]{1,0:T(4,128)} %box_ref.1, f32[24]{0:T(128)} %occ_ref.1, f32[13,13]{1,0:T(8,128)} %coup_ref.1, bf16[24,16,16,128]{3,2,1,0:T(8,128)(2,1)} %orb_hbm.1, ...), custom_call_target="tpu_custom_call" | custom-call | tf_op jit(solution)/shard_map/pallas_call | solution.py:593
  35.0 2.8 %shard_map.114 = (bf16[24,16,16,128]{3,2,1,0:T(8,128)(2,1)}, f32[16,16,128]{2,1,0:T(8,128)}) custom-call(f32[24,256,128]{2,1,0:T(8,128)S(1)} %get-tuple-element.7.local_part, f32[6144,128]{1,0:T(8,128)S(1)} %get-tuple-element.8.nonlocal_part, bf16[2,24,2,16,128]{4,3,2,1,0:T(8,128)(2,1)S(1)} %get-tuple-element.9.halo, ...), custom_call_target="tpu_custom_call" | custom-call | tf_op jit(solution)/shard_map/pallas_call | solution.py:620

commit v6 on v5

--- a/solution.py
+++ b/solution.py
@@ -462,19 +462,34 @@
     halo,
     charge_ref,
     pre_ref,
+    ion_hbm,
+    app_hbm,
+    pot_hbm,
+    app_ref,
     ion_ref,
-    app_hbm,
     pot_ref,
-    app_ref,
     s_app,
+    s_pot,
 ):
     orbs, planes, rows, cols = app_ref.shape
     cells = planes * rows
     batches = s_app.shape[0]
     some = orbs // batches
     scale = -0.5 / 12.0
+    load = pltpu.make_async_copy(ion_hbm, ion_ref, s_pot.at[0])
+    load.start()
     outs = []
     for n in range(batches):
+        if n == batches // 2:
+            inverse = 1.0 / (6.0 + SCREENING)
+            total = jnp.sum(charge_ref[...], axis=(0, 1), keepdims=True)
+            mean = total * (1.0 / (cells * cols * n_space))
+            lift = FOUR_PI * inverse * (1.0 + 6.0 * inverse) * mean
+            load.wait()
+            for p in range(planes):
+                pot_ref[p] = ion_ref[p] + (pre_ref[p] - lift)
+            outs.append(pltpu.make_async_copy(pot_ref, pot_hbm, s_pot.at[1]))
+            outs[-1].start()
         for o in range(n * some, (n + 1) * some):
             near_low, far_low = halo[0, o, 1].astype(F32), halo[0, o, 0].astype(F32)
             near_up, far_up = halo[1, o, 0].astype(F32), halo[1, o, 1].astype(F32)
@@ -493,13 +508,7 @@
                 app_ref[o, i] = total.astype(BF16)
         at = pl.ds(n * some, some)
         outs.append(pltpu.make_async_copy(app_ref.at[at], app_hbm.at[at], s_app.at[n]))
-        outs[n].start()
-
-    inverse = 1.0 / (6.0 + SCREENING)
-    mean = jnp.sum(charge_ref[...], axis=(0, 1), keepdims=True) * (1.0 / (cells * cols * n_space))
-    lift = FOUR_PI * inverse * (1.0 + 6.0 * inverse) * mean
-    for p in range(planes):
-        pot_ref[p] = ion_ref[p] + (pre_ref[p] - lift)
+        outs[-1].start()
     for copy in outs:
         copy.wait()
 
@@ -620,9 +629,15 @@
     return pl.pallas_call(
         functools.partial(finish_terms, n_space),
         out_shape=(jax.ShapeDtypeStruct(orbitals.shape, BF16), grid_f32),
-        in_specs=[vmem] * 6,
-        out_specs=(anywhere, vmem),
-        scratch_shapes=[pltpu.VMEM(orbitals.shape, BF16), dma((4,))],
+        in_specs=[vmem] * 5 + [anywhere],
+        out_specs=(anywhere, anywhere),
+        scratch_shapes=[
+            pltpu.VMEM(orbitals.shape, BF16),
+            pltpu.VMEM(potential_in.shape, F32),
+            pltpu.VMEM(potential_in.shape, F32),
+            dma((6,)),
+            dma((2,)),
+        ],
         compiler_params=pltpu.CompilerParams(vmem_limit_bytes=54 * 1024 * 1024),
     )(*handed, ionic_potential)
 

time: 38.3 us -> 37.4 us (0.977)
  Pallas kernels: 37.1 us -> 36.3 us
    pallas_call x1, Pallas kernels: 2.83 us -> 1.95 us  [local(): pl.pallas_call(functools.partial(finish_terms, n_space), out_shape=(jax.S...]
where the time goes in v6:
time: 37.4 us; the launch traced here: 36.9 us
  Pallas kernels  36.3 us (97%)
  between operations  0.64 us (2%)
    pallas_call x1, Pallas kernels, local(): pl.pallas_call(functools.partial(exchange, (n_band, n_space, group)), out...  34.3 us
    pallas_call x1, Pallas kernels, local(): pl.pallas_call(functools.partial(finish_terms, n_space), out_shape=(jax.S...  1.95 us

profile of v6, /device:TPU:24, one launch (start us, length us, event | category | flops | bytes accessed | tf_op | source)
XLA Modules:
  0.0 36.9 jit_solution(12696661191671189595)
XLA Ops:
  0.6 34.3 %shard_map.113 = (f32[24,256,128]{2,1,0:T(8,128)S(1)}, f32[6144,128]{1,0:T(8,128)S(1)}, bf16[2,24,2,16,128]{4,3,2,1,0:T(8,128)(2,1)S(1)}, f32[8,128]{1,0:T(8,128)S(1)}, f32[16,16,128]{2,1,0:T(8,128)S(1)}) custom-call(s32[3,512]{1,0:T(4,128)} %box_ref.1, f32[24]{0:T(128)} %occ_ref.1, f32[13,13]{1,0:T(8,128)} %coup_ref.1, bf16[24,16,16,128]{3,2,1,0:T(8,128)(2,1)} %orb_hbm.1, ...), custom_call_target="tpu_custom_call" | custom-call | tf_op jit(solution)/shard_map/pallas_call | solution.py:602
  35.0 2.0 %shard_map.114 = (bf16[24,16,16,128]{3,2,1,0:T(8,128)(2,1)}, f32[16,16,128]{2,1,0:T(8,128)}) custom-call(f32[24,256,128]{2,1,0:T(8,128)S(1)} %get-tuple-element.7.local_part, f32[6144,128]{1,0:T(8,128)S(1)} %get-tuple-element.8.nonlocal_part, bf16[2,24,2,16,128]{4,3,2,1,0:T(8,128)(2,1)S(1)} %get-tuple-element.9.halo, ...), custom_call_target="tpu_custom_call" | custom-call | tf_op jit(solution)/shard_map/pallas_call | solution.py:629

commit v7 on v6

--- a/solution.py
+++ b/solution.py
@@ -302,99 +302,6 @@
 
     hand_on(1)
 
-    for d in range(1, group):
-        peer = lax.rem(near + d, group)
-        arrived(chg_in2.at[peer], s_c2.at[d], r_c2.at[peer])
-    charge = chg1[...]
-    for d in range(1, group):
-        charge = charge + chg_in2[lax.rem(near + d, group)]
-    chg2[...] = charge
-    for d in range(1, n_far):
-        send(chg2, chg_in3.at[far], s_c3.at[d], r_c3.at[far], far_peer(d))
-    send(orb_ref.at[:, pl.ds(planes - 2, 2)], halo.at[0], s_halo.at[0], r_halo.at[0], (me_b, nxt))
-
-    for n in range(2, 5):
-        loads[n].wait()
-    for pair in range(orbs // 2):
-        if pair == orbs // 4:
-            hand_across(0)
-        first, second = orb_ref[2 * pair], orb_ref[2 * pair + 1]
-        both = jnp.concatenate([first.reshape(cells, cols), second.reshape(cells, cols)], axis=1)
-        lap = jnp.dot(left_ref[...], both, preferred_element_type=F32)
-        lap = lap + jnp.dot(both, right_ref[...], preferred_element_type=F32)
-        vin = vin_ref[...].reshape(cells, cols)
-        for n in range(2):
-            field = both[:, n * cols : (n + 1) * cols].astype(F32)
-            local_part[2 * pair + n] = lap[:, n * cols : (n + 1) * cols] * (-0.5 / 12.0) + vin * field
-    hand_across(1)
-
-    for d in range(1, n_band):
-        peer = lax.rem(me_b + d, n_band)
-        arrived(dens_in.at[peer], s_dens.at[d], r_dens.at[peer])
-    total_density = dens_f[...]
-    for d in range(1, n_band):
-        total_density = total_density + dens_in[lax.rem(me_b + d, n_band)].astype(F32)
-    rho[...] = total_density
-    send(rho.at[0], rhalo.at[1], s_rh.at[1], r_rh.at[1], (me_b, prv))
-    send(rho.at[planes - 1], rhalo.at[0], s_rh.at[0], r_rh.at[0], (me_b, nxt))
-    for d in range(1, n_far):
-        peer = lax.rem(far + d, n_far)
-        arrived(chg_in3.at[peer], s_c3.at[d], r_c3.at[peer])
-    charge = chg2[...]
-    for d in range(1, n_far):
-        charge = charge + chg_in3[lax.rem(far + d, n_far)]
-    chg3[...] = charge
-    for d in range(1, n_band):
-        send(chg3, chg_in1.at[me_b], s_c1.at[d], r_c1.at[me_b], band_peer(d))
-
-    for base in (me_b, across):
-        for h in range(share):
-            gather(1, pprev, first_prev, base * share + h)
-    for base, send_sem, recv_sem in ((sib, s_fwd, r_fwd), (beyond, s_last, r_last)):
-        for h in range(share):
-            a = base * share + h
-            arrived(pprev.at[a], send_sem.at[h], recv_sem.at[h])
-            gather(1, pprev, first_prev, a)
-    part_prev[...] = gathered_sum()
-    send(part_prev, got_own, s_part.at[1], r_part.at[1], (me_b, prv))
-
-    loads[5].wait()
-    for side in range(2):
-        arrived(hhalo.at[side], s_hh.at[side], r_hh.at[side])
-        arrived(rhalo.at[side], s_rh.at[side], r_rh.at[side])
-
-    def around(cell):
-        return (
-            pltpu.roll(cell, 1, 0)
-            + pltpu.roll(cell, rows - 1, 0)
-            + pltpu.roll(cell, 1, 1)
-            + pltpu.roll(cell, cols - 1, 1)
-        )
-
-    def start_plane(p):
-        if p < 0:
-            return hhalo[0, p + 2]
-        if p >= planes:
-            return hhalo[1, p - planes]
-        return har_ref[p]
-
-    def rho_plane(p):
-        if p < 0:
-            return rhalo[0]
-        if p >= planes:
-            return rhalo[1]
-        return rho[p]
-
-    inverse = 1.0 / (6.0 + SCREENING)
-    for p in range(-1, planes + 1):
-        total = start_plane(p - 1) + start_plane(p + 1) + around(start_plane(p))
-        hone[p + 1] = (total + FOUR_PI * rho_plane(p)) * inverse
-    for p in range(planes):
-        total = hone[p] + hone[p + 2] + around(hone[p + 1])
-        second = (total + FOUR_PI * rho[p]) * inverse
-        root = jnp.exp(jnp.log(rho[p] * (3.0 / math.pi)) * (1.0 / 3.0))
-        pre_ref[p] = second - root
-
     row_id = lax.broadcasted_iota(jnp.int32, (cols, nproj), 0) % nproj
     pick = jnp.where(
         row_id == lax.broadcasted_iota(jnp.int32, (cols, nproj), 1), 1.0, 0.0
@@ -415,9 +322,106 @@
     )
     couple[...] = jnp.where(same, full, 0.0)
 
-    arrived(got_prev, s_part.at[0], r_part.at[0])
-    arrived(got_own, s_part.at[1], r_part.at[1])
-    for part, mine, other in ((0, part_own, got_own), (1, part_prev, got_prev)):
+    for d in range(1, group):
+        peer = lax.rem(near + d, group)
+        arrived(chg_in2.at[peer], s_c2.at[d], r_c2.at[peer])
+    charge = chg1[...]
+    for d in range(1, group):
+        charge = charge + chg_in2[lax.rem(near + d, group)]
+    chg2[...] = charge
+    for d in range(1, n_far):
+        send(chg2, chg_in3.at[far], s_c3.at[d], r_c3.at[far], far_peer(d))
+    send(orb_ref.at[:, pl.ds(planes - 2, 2)], halo.at[0], s_halo.at[0], r_halo.at[0], (me_b, nxt))
+
+    for h in range(share):
+        gather(1, pprev, first_prev, me_b * share + h)
+
+    for n in range(2, 5):
+        loads[n].wait()
+    for pair in range(orbs // 2):
+        if pair == orbs // 4:
+            hand_across(0)
+        first, second = orb_ref[2 * pair], orb_ref[2 * pair + 1]
+        both = jnp.concatenate([first.reshape(cells, cols), second.reshape(cells, cols)], axis=1)
+        lap = jnp.dot(left_ref[...], both, preferred_element_type=F32)
+        lap = lap + jnp.dot(both, right_ref[...], preferred_element_type=F32)
+        vin = vin_ref[...].reshape(cells, cols)
+        for n in range(2):
+            field = both[:, n * cols : (n + 1) * cols].astype(F32)
+            local_part[2 * pair + n] = lap[:, n * cols : (n + 1) * cols] * (-0.5 / 12.0) + vin * field
+    hand_across(1)
+    for h in range(share):
+        gather(1, pprev, first_prev, across * share + h)
+
+    for d in range(1, n_band):
+        peer = lax.rem(me_b + d, n_band)
+        arrived(dens_in.at[peer], s_dens.at[d], r_dens.at[peer])
+    total_density = dens_f[...]
+    for d in range(1, n_band):
+        total_density = total_density + dens_in[lax.rem(me_b + d, n_band)].astype(F32)
+    rho[...] = total_density
+    send(rho.at[0], rhalo.at[1], s_rh.at[1], r_rh.at[1], (me_b, prv))
+    send(rho.at[planes - 1], rhalo.at[0], s_rh.at[0], r_rh.at[0], (me_b, nxt))
+    for base, send_sem, recv_sem in ((sib, s_fwd, r_fwd), (beyond, s_last, r_last)):
+        for h in range(share):
+            a = base * share + h
+            arrived(pprev.at[a], send_sem.at[h], recv_sem.at[h])
+            gather(1, pprev, first_prev, a)
+    part_prev[...] = gathered_sum()
+    send(part_prev, got_own, s_part.at[1], r_part.at[1], (me_b, prv))
+
+    for d in range(1, n_far):
+        peer = lax.rem(far + d, n_far)
+        arrived(chg_in3.at[peer], s_c3.at[d], r_c3.at[peer])
+    charge = chg2[...]
+    for d in range(1, n_far):
+        charge = charge + chg_in3[lax.rem(far + d, n_far)]
+    chg3[...] = charge
+    for d in range(1, n_band):
+        send(chg3, chg_in1.at[me_b], s_c1.at[d], r_c1.at[me_b], band_peer(d))
+
+    loads[5].wait()
+    for side in range(2):
+        arrived(hhalo.at[side], s_hh.at[side], r_hh.at[side])
+        arrived(rhalo.at[side], s_rh.at[side], r_rh.at[side])
+
+    def around(cell):
+        return (
+            pltpu.roll(cell, 1, 0)
+            + pltpu.roll(cell, rows - 1, 0)
+            + pltpu.roll(cell, 1, 1)
+            + pltpu.roll(cell, cols - 1, 1)
+        )
+
+    def start_plane(p):
+        if p < 0:
+            return hhalo[0, p + 2]
+        if p >= planes:
+            return hhalo[1, p - planes]
+        return har_ref[p]
+
+    def rho_plane(p):
+        if p < 0:
+            return rhalo[0]
+        if p >= planes:
+            return rhalo[1]
+        return rho[p]
+
+    inverse = 1.0 / (6.0 + SCREENING)
+    for p in range(-1, planes + 1):
+        total = start_plane(p - 1) + start_plane(p + 1) + around(start_plane(p))
+        hone[p + 1] = (total + FOUR_PI * rho_plane(p)) * inverse
+    for p in range(planes):
+        total = hone[p] + hone[p + 2] + around(hone[p + 1])
+        second = (total + FOUR_PI * rho[p]) * inverse
+        root = jnp.exp(jnp.log(rho[p] * (3.0 / math.pi)) * (1.0 / 3.0))
+        pre_ref[p] = second - root
+
+    for part, mine, other, first in (
+        (1, part_prev, got_prev, first_prev),
+        (0, part_own, got_own, first_own),
+    ):
+        arrived(other, s_part.at[1 - part], r_part.at[1 - part])
         weighted = lax.dot_general(
             couple[...],
             mine[...] + other[...],
@@ -426,17 +430,15 @@
             preferred_element_type=F32,
         ).astype(BF16)
         weights[part] = jnp.dot(weighted, belongs, preferred_element_type=F32)
-
-    for n in range(2 * atoms):
-        part, a = n // atoms, n % atoms
-        first = (first_own, first_prev)[part]
-        keep = step == lax.rem(box_ref[0, first + a], planes) - part * planes
-        rows_a = weights[part, a * nproj : (a + 1) * nproj, :].reshape(nproj, 1, wide)
-        placed = jnp.where(keep[None], rows_a, 0.0)
-        placed = placed.reshape(nproj * width, wide).astype(BF16)
-        term = jnp.dot(turned[n], placed, preferred_element_type=F32).astype(BF16)
-        for y in range(rows):
-            added[y, n * SLOT : (n + 1) * SLOT, :] = term[y * SLOT : (y + 1) * SLOT, :]
+        for a in range(atoms):
+            n = part * atoms + a
+            keep = step == lax.rem(box_ref[0, first + a], planes) - part * planes
+            rows_a = weights[part, a * nproj : (a + 1) * nproj, :].reshape(nproj, 1, wide)
+            placed = jnp.where(keep[None], rows_a, 0.0)
+            placed = placed.reshape(nproj * width, wide).astype(BF16)
+            term = jnp.dot(turned[n], placed, preferred_element_type=F32).astype(BF16)
+            for y in range(rows):
+                added[y, n * SLOT : (n + 1) * SLOT, :] = term[y * SLOT : (y + 1) * SLOT, :]
     for y in range(rows):
         fields[pl.ds(y, wide, stride=rows), :] = lax.dot_general(
             added[y], scat[...], (((0,), (0,)), ((), ())), preferred_element_type=F32

time: 37.4 us -> 37.5 us (level)
  no operation moved by 1% of the time
where the time goes in v7:
time: 37.5 us; the launch traced here: 36.9 us
  Pallas kernels  36.2 us (97%)
  between operations  0.64 us (2%)
    pallas_call x1, Pallas kernels, local(): pl.pallas_call(functools.partial(exchange, (n_band, n_space, group)), out...  34.3 us
    pallas_call x1, Pallas kernels, local(): pl.pallas_call(functools.partial(finish_terms, n_space), out_shape=(jax.S...  1.95 us

profile of v7, /device:TPU:24, one launch (start us, length us, event | category | flops | bytes accessed | tf_op | source)
XLA Modules:
  0.0 36.9 jit_solution(7669774452549752014)
XLA Ops:
  0.6 34.3 %shard_map.113 = (f32[24,256,128]{2,1,0:T(8,128)S(1)}, f32[6144,128]{1,0:T(8,128)S(1)}, bf16[2,24,2,16,128]{4,3,2,1,0:T(8,128)(2,1)S(1)}, f32[8,128]{1,0:T(8,128)S(1)}, f32[16,16,128]{2,1,0:T(8,128)S(1)}) custom-call(s32[3,512]{1,0:T(4,128)} %box_ref.1, f32[24]{0:T(128)} %occ_ref.1, f32[13,13]{1,0:T(8,128)} %coup_ref.1, bf16[24,16,16,128]{3,2,1,0:T(8,128)(2,1)} %orb_hbm.1, ...), custom_call_target="tpu_custom_call" | custom-call | tf_op jit(solution)/shard_map/pallas_call | solution.py:604
  34.9 2.0 %shard_map.114 = (bf16[24,16,16,128]{3,2,1,0:T(8,128)(2,1)}, f32[16,16,128]{2,1,0:T(8,128)}) custom-call(f32[24,256,128]{2,1,0:T(8,128)S(1)} %get-tuple-element.7.local_part, f32[6144,128]{1,0:T(8,128)S(1)} %get-tuple-element.8.nonlocal_part, bf16[2,24,2,16,128]{4,3,2,1,0:T(8,128)(2,1)S(1)} %get-tuple-element.9.halo, ...), custom_call_target="tpu_custom_call" | custom-call | tf_op jit(solution)/shard_map/pallas_call | solution.py:631

commit v8 on v7

--- a/solution.py
+++ b/solution.py
@@ -80,6 +80,7 @@
     left_ref,
     right_ref,
     pprev,
+    relay,
     hhalo,
     rhalo,
     dens_f,
@@ -129,6 +130,8 @@
     r_rh,
     s_part,
     r_part,
+    s_relay,
+    r_relay,
 ):
     n_band, n_space, group = dims
     orbs, planes, rows, cols = orb_ref.shape
@@ -239,8 +242,6 @@
         send_projectors(h)
     for d in range(1, n_band):
         send(dens_b, dens_in.at[me_b], s_dens.at[d], r_dens.at[me_b], band_peer(d))
-
-    send(orb_ref.at[:, pl.ds(0, 2)], halo.at[1], s_halo.at[1], r_halo.at[1], (me_b, prv))
 
     for y in range(rows):
         line = fields[pl.ds(y, wide, stride=rows), :].astype(BF16)
@@ -331,7 +332,26 @@
     chg2[...] = charge
     for d in range(1, n_far):
         send(chg2, chg_in3.at[far], s_c3.at[d], r_c3.at[far], far_peer(d))
-    send(orb_ref.at[:, pl.ds(planes - 2, 2)], halo.at[0], s_halo.at[0], r_halo.at[0], (me_b, nxt))
+    at_end = jnp.logical_and(far == n_far - 1, lax.rem(near, 4) == 2)
+    on_way = jnp.logical_and(far == n_far - 1, lax.rem(near, 4) == 3)
+
+    def planes_up(src, dst, send_sem, recv_sem, device):
+        return pltpu.make_async_remote_copy(
+            src_ref=src,
+            dst_ref=dst,
+            send_sem=send_sem,
+            recv_sem=recv_sem,
+            device_id=device,
+            device_id_type=MESH,
+        )
+
+    upper = orb_ref.at[:, pl.ds(planes - 2, 2)]
+    straight = planes_up(upper, halo.at[0], s_halo.at[0], r_halo.at[0], (me_b, nxt))
+    turning = planes_up(upper, relay, s_halo.at[0], r_relay, near_peer(1))
+    onward = planes_up(relay, halo.at[0], s_relay, r_halo.at[0], far_peer(1))
+    pl.when(jnp.logical_not(at_end))(straight.start)
+    pl.when(at_end)(turning.start)
+
 
     for h in range(share):
         gather(1, pprev, first_prev, me_b * share + h)
@@ -349,9 +369,15 @@
         for n in range(2):
             field = both[:, n * cols : (n + 1) * cols].astype(F32)
             local_part[2 * pair + n] = lap[:, n * cols : (n + 1) * cols] * (-0.5 / 12.0) + vin * field
+    send(orb_ref.at[:, pl.ds(0, 2)], halo.at[1], s_halo.at[1], r_halo.at[1], (me_b, prv))
     hand_across(1)
     for h in range(share):
         gather(1, pprev, first_prev, across * share + h)
+
+    @pl.when(on_way)
+    def _():
+        turning.wait_recv()
+        onward.start()
 
     for d in range(1, n_band):
         peer = lax.rem(me_b + d, n_band)
@@ -455,6 +481,8 @@
         arrived(halo.at[side], s_halo.at[side], r_halo.at[side])
     for copy in sent:
         copy.wait_send()
+    straight.wait_send()
+    pl.when(on_way)(onward.wait_send)
 
 
 def finish_terms(
@@ -551,6 +579,7 @@
         pltpu.VMEM(left.shape, BF16),
         pltpu.VMEM(right.shape, BF16),
         pltpu.VMEM(projectors.shape, BF16),
+        pltpu.VMEM(halo_shape[1:], BF16),
         pltpu.VMEM((2, 2, rows, cols), F32),
         pltpu.VMEM((2, rows, cols), F32),
         pltpu.VMEM((planes, rows, cols), F32),
@@ -600,6 +629,8 @@
         dma((2,)),
         dma((2,)),
         dma((2,)),
+        dma,
+        dma,
     ]
     handed = pl.pallas_call(
         functools.partial(exchange, (n_band, n_space, group)),

time: 37.5 us -> 37.6 us (level)
  no operation moved by 1% of the time
where the time goes in v8:
time: 37.6 us; the launch traced here: 36.9 us
  Pallas kernels  36.2 us (96%)
  between operations  0.64 us (2%)
    pallas_call x1, Pallas kernels, local(): pl.pallas_call(functools.partial(exchange, (n_band, n_space, group)), out...  34.3 us
    pallas_call x1, Pallas kernels, local(): pl.pallas_call(functools.partial(finish_terms, n_space), out_shape=(jax.S...  1.95 us

profile of v8, /device:TPU:24, one launch (start us, length us, event | category | flops | bytes accessed | tf_op | source)
XLA Modules:
  0.0 36.9 jit_solution(13849673275478810220)
XLA Ops:
  0.6 34.3 %shard_map.113 = (f32[24,256,128]{2,1,0:T(8,128)S(1)}, f32[6144,128]{1,0:T(8,128)S(1)}, bf16[2,24,2,16,128]{4,3,2,1,0:T(8,128)(2,1)S(1)}, f32[8,128]{1,0:T(8,128)S(1)}, f32[16,16,128]{2,1,0:T(8,128)S(1)}) custom-call(s32[3,512]{1,0:T(4,128)} %box_ref.1, f32[24]{0:T(128)} %occ_ref.1, f32[13,13]{1,0:T(8,128)} %coup_ref.1, bf16[24,16,16,128]{3,2,1,0:T(8,128)(2,1)} %orb_hbm.1, ...), custom_call_target="tpu_custom_call" | custom-call | tf_op jit(solution)/shard_map/pallas_call | solution.py:635
  34.9 2.0 %shard_map.114 = (bf16[24,16,16,128]{3,2,1,0:T(8,128)(2,1)}, f32[16,16,128]{2,1,0:T(8,128)}) custom-call(f32[24,256,128]{2,1,0:T(8,128)S(1)} %get-tuple-element.7.local_part, f32[6144,128]{1,0:T(8,128)S(1)} %get-tuple-element.8.nonlocal_part, bf16[2,24,2,16,128]{4,3,2,1,0:T(8,128)(2,1)S(1)} %get-tuple-element.9.halo, ...), custom_call_target="tpu_custom_call" | custom-call | tf_op jit(solution)/shard_map/pallas_call | solution.py:662
